TPU v7x, 512 devices: a whole 4x8x8 slice. The times are simulated.
512 devices in a mesh: trade: 64 (over x, y, core), scen: 8 (over z).
Axes of the slice: x: 4, y: 8, z: 8, core: 2. Of those that a mesh axis runs over, the one named last changes fastest.
Arguments:
- draws: bfloat16 [8, 512, 4096], P('scen', 'trade'), may hold values from -5 to 5
- loadings: bfloat16 [4096, 4096], P('trade'), may hold values from -0.09375 to 0.09375
- base_yield: float32 [4096], P('trade'), may hold values from 0.005 to 0.06
- cashflows: bfloat16 [64, 131072], P(None, 'trade'), may hold values from -0.3125 to 0.3125
- netting_id: int32 [131072], P('trade'), may hold values from 0 to 1023
- live_trades: int32 [64], P('trade'), may hold values from 1 to 2048, 78643 in all
- dist_prev: float32 [1024, 4096], P('trade', 'scen'), may hold values from -0.15 to 0.6
- shock: float32 [1024, 4096], P('trade', 'scen'), may hold values from -5 to 5
- vol: float32 [1024], P('trade'), may hold values from 0.2 to 0.8
Outputs:
- net_value: float32 [1024, 4096], P('trade', 'scen')
- expected_loss: float32 [1024], P('trade')
All inputs are finite; a program needn't handle non-finite values. No bound on the sum of `live_trades` on one device may be relied on, other than what follows from the above.
Results may differ from a plain program's by a relative error of at most 0.003.
Values may be sent and summed in bfloat16 or wider, within the bound.
No kernel may reach another device: no remote copies, remote signals or barrier semaphores. Data moves between devices by JAX's collectives and lax.ppermute only.
A program may use at most 64 MiB of HBM per device.

v0:
```python
import jax
import jax.numpy as jnp
from jax import lax
from jax.sharding import PartitionSpec as P


def body(draws, loadings, base_yield, cashflows, netting_id, live_trades, dist_prev, shock, vol):
    pillars = loadings.shape[0]
    factors = lax.dot_general(
        loadings,
        lax.all_gather(draws, "trade", axis=1, tiled=True)[0],
        (((1,), (1,)), ((), ())),
        preferred_element_type=jnp.float32,
    )
    tenors = (jnp.arange(pillars, dtype=jnp.int32) + 1).astype(jnp.float32) * (16.0 / pillars)
    discount = jnp.exp(-tenors[:, None] * (base_yield[:, None] + 0.02 * factors)).astype(
        jnp.bfloat16
    )
    scen_rows = discount.shape[1]
    owned = dist_prev.shape[0]
    groups = lax.axis_size("trade")
    set_total = owned * groups
    trades = cashflows.shape[1]
    block_rows = min(2048, trades)
    live_count = live_trades[0]
    set_numbers = jnp.arange(set_total, dtype=jnp.int32)

    def price_block(block, totals):
        first = block * block_rows
        alive = first + jnp.arange(block_rows, dtype=jnp.int32) < live_count
        member = jnp.where(
            (netting_id[None, :] == set_numbers[:, None]) & alive[None, :], 1.0, 0.0
        ).astype(jnp.bfloat16)
        return totals + lax.dot_general(
            cashflows, member, (((1,), (1,)), ((), ())), preferred_element_type=jnp.float32
        )

    steps_run = trades // block_rows
    set_flows = lax.fori_loop(
        0, steps_run, price_block, jnp.zeros((pillars, set_total), jnp.float32)
    )
    partial_value = lax.dot_general(
        set_flows,
        discount.astype(jnp.float32),
        (((0,), (0,)), ((), ())),
        precision=lax.Precision.HIGHEST,
        preferred_element_type=jnp.float32,
    )
    whole = lax.psum(partial_value, "trade")
    net_value = lax.dynamic_slice_in_dim(whole, lax.axis_index("trade") * owned, owned, 0)
    spread = vol[:, None]
    dist_now = dist_prev + (0.03 - 0.5 * spread * spread) + spread * shock
    crossing = jnp.exp(
        -2.0 * jnp.maximum(dist_prev, 0.0) * jnp.maximum(dist_now, 0.0) / (spread * spread)
    )
    losses = jnp.maximum(net_value, 0.0) * crossing
    summed = lax.psum(jnp.sum(losses, axis=1), "scen")
    expected_loss = summed / (scen_rows * lax.axis_size("scen"))
    return (net_value, expected_loss)


def solution(mesh):
    in_specs = (
        P("scen", "trade", None),
        P("trade", None),
        P("trade"),
        P(None, "trade"),
        P("trade"),
        P("trade"),
        P("trade", "scen"),
        P("trade", "scen"),
        P("trade"),
    )
    out_specs = (P("trade", "scen"), P("trade"))
    return jax.shard_map(body, mesh=mesh, in_specs=in_specs, out_specs=out_specs, check_vma=False)
```

profile of v0, /device:TPU:6, one launch (start us, length us, event | category | flops | bytes accessed | tf_op | source)
XLA Modules:
  0.0 329.7 jit_solution(8959349385118430116)
XLA Ops:
  7.2 0.0 copy-start
  7.2 0.0 all-gather.2.cloned.1.call-start
  7.2 0.7 all-gather.2.cloned.1.call-update
  7.9 0.0 all-reduce.2.cloned.1.call-start
  8.6 0.0 copy-start.4
  8.6 2.4 fusion.3
  11.0 0.0 copy-start.3
  11.1 0.0 copy-start.1
  11.1 0.0 copy-start.2
  11.1 87.7 %all-gather.2.cloned.1.call-done = bf16[1,512,4096]{2,1,0:T(8,128)(2,1)} async-done(((bf16[1,8,4096]{2,1,0:T(8,128)(2,1)}), bf16[1,512,4096]{2,1,0:T(8,128)(2,1)}) %all-gather.2.cloned.1.call-update) | async-done | bytes 4194320 | tf_op jit(solution)/shard_map/all_gather | solution.py:11
  98.8 0.0 copy-done
  98.8 0.0 copy-done.4
  98.8 3.6 %fusion.17 = bf16[64,512]{1,0:T(8,128)(2,1)S(1)} fusion(bf16[64,4096]{1,0:T(8,128)(2,1)S(1)} %copy-done, bf16[1,512,4096]{2,1,0:T(8,128)(2,1)} %all-gather.2.cloned.1.call-done, f32[64]{0:T(128)S(1)} %copy-done.4, f32[64]{0:T(128)S(1)} %multiply_negate_fusion), kind=kOutput, calls=%fused_computation.11 | convolution fusion | flops 268566528 | bytes 4784640 | tf_op jit(solution)/shard_map/dot_general | solution.py:9
  102.4 2.3 fusion.23
  104.7 0.0 all-reduce.2.cloned.1.call-update
  104.7 0.0 copy-done.3
  104.7 198.0 %all-reduce.2.cloned.1.call-done = f32[1024,512]{1,0:T(8,128)} async-done(((f32[1024,512]{1,0:T(8,128)}), f32[1024,512]{1,0:T(8,128)}) %all-reduce.2.cloned.1.call-update) | async-done | bytes 2097168 | tf_op jit(solution)/shard_map/psum | solution.py:49
  302.7 0.0 copy-done.1
  302.7 0.0 copy-done.2
  302.7 1.5 multiply_reduce_fusion
  304.2 18.1 %psum.15 = f32[16]{0:T(128)S(1)} all-reduce(f32[16]{0:T(128)S(1)} %get-tuple-element.16), channel_id=1, replica_groups=mesh['trade'=64,'scen'=8] {'scen'}, use_global_device_ids=true, to_apply=%region_2.3 | all-reduce | flops 16 | bytes 128 | tf_op jit(solution)/shard_map/psum | solution.py:57
  322.3 0.5 broadcast_multiply_fusion
  (3 shorter events, 0.0 us)
Async XLA Ops:
  7.2 91.6 %copy-start = (bf16[64,4096]{1,0:T(8,128)(2,1)S(1)}, bf16[64,4096]{1,0:T(8,128)(2,1)}, u32[]{:S(2)}) copy-start(bf16[64,4096]{1,0:T(8,128)(2,1)} %param.10) | copy-start | bytes 1572868
  7.2 91.6 %all-gather.2.cloned.1.call-start = ((), (), s32[]{:S(2)}) async-start(), calls=%async_computation | async-start | bytes 4259840 | tf_op jit(solution)/shard_map/all_gather | solution.py:11
  7.9 294.8 %all-reduce.2.cloned.1.call-start = ((), (), s32[]{:S(2)}) async-start(), calls=%async_computation.1 | async-start | bytes 4194304 | tf_op jit(solution)/shard_map/psum | solution.py:49
  8.6 90.2 %copy-start.4 = (f32[64]{0:T(128)S(1)}, f32[64]{0:T(128)}, u32[]{:S(2)}) copy-start(f32[64]{0:T(128)} %param.11) | copy-start | bytes 772
  11.0 93.7 %copy-start.3 = (f32[16]{0:T(128)S(1)}, f32[16]{0:T(128)}, u32[]{:S(2)}) copy-start(f32[16]{0:T(128)} %param.17) | copy-start | bytes 196
  11.1 291.7 %copy-start.1 = (f32[16,512]{1,0:T(8,128)S(1)}, f32[16,512]{1,0:T(8,128)}, u32[]{:S(2)}) copy-start(f32[16,512]{1,0:T(8,128)} %param.16) | copy-start | bytes 98308
  11.1 291.7 %copy-start.2 = (f32[16,512]{1,0:T(8,128)S(1)}, f32[16,512]{1,0:T(8,128)}, u32[]{:S(2)}) copy-start(f32[16,512]{1,0:T(8,128)} %param.15) | copy-start | bytes 98308
Sparse Core Ops, SparseCore 0:
  11.4 87.3 all-gather.1
  104.8 197.8 all-reduce.1
where the time goes:
time: 331 us; the launch traced here: 330 us
  waiting for transfers between devices  286 us (86%)
  blocking collectives  18.1 us (5%)
  between operations  14.8 us (4%)
  matrix products  8.26 us (2%)
    psum x1, waiting for transfers between devices, body(): whole = lax.psum(partial_value, 'trade')  198 us
    all_gather x1, waiting for transfers between devices, body(): lax.all_gather(draws, 'trade', axis=1, tiled=True)[0]  87.7 us
    psum x1, blocking collectives, body(): summed = lax.psum(jnp.sum(losses, axis=1), 'scen')  18.1 us
  transfers between devices with their start and end apart: 2, of which 2 were waited for; matrix products, arithmetic and copies ran while one was open for 1% of the time, Pallas kernels for 0%

commit v1 on v0

v1 whole, which is shorter than its diff:
```python
import jax
import jax.numpy as jnp
from jax import lax
from jax.sharding import Mesh, PartitionSpec as P

TRADE = ("x", "y", "core")


def shift(value, axis, by):
    size = lax.axis_size(axis)
    return lax.ppermute(value, axis, [(i, (i + by) % size) for i in range(size)])


def everywhere(value, axis):
    size = lax.axis_size(axis)
    copies = jnp.broadcast_to(value[None], (size, *value.shape))
    return lax.all_to_all(copies, axis, 0, 0, tiled=True)


def netting_flows(cashflows, netting_id, live_count, set_total):
    trades = cashflows.shape[1]
    alive = jnp.arange(trades, dtype=jnp.int32) < live_count
    set_numbers = jnp.arange(set_total, dtype=jnp.int32)
    member = jnp.where(
        (netting_id[None, :] == set_numbers[:, None]) & alive[None, :], 1.0, 0.0
    ).astype(jnp.bfloat16)
    return lax.dot_general(
        cashflows, member, (((1,), (1,)), ((), ())), preferred_element_type=jnp.float32
    )


def body(draws, loadings, base_yield, cashflows, netting_id, live_trades, dist_prev, shock, vol):
    pillars = loadings.shape[0]
    owned, scen_rows = dist_prev.shape
    quarters = lax.axis_size("x")
    groups = quarters * lax.axis_size("y") * lax.axis_size("core")
    set_total = owned * groups
    part = scen_rows // quarters

    flows = netting_flows(cashflows, netting_id, live_trades[0], set_total)
    packed = jnp.concatenate(
        [flows, jnp.broadcast_to(base_yield[:, None], (pillars, 128))], axis=1
    )
    shifts = (1, -1, 2)
    loads = [loadings] + [shift(loadings, "x", by) for by in shifts]
    packs = [packed] + [shift(packed, "x", by) for by in shifts]

    mine = everywhere(draws[0], "y")
    other = shift(mine, "core", 1)
    first = lax.axis_index("core") == 0
    normals = jnp.where(
        first, jnp.stack([mine, other], axis=1), jnp.stack([other, mine], axis=1)
    ).reshape(part, -1)

    tenors = (jnp.arange(pillars, dtype=jnp.int32) + 1).astype(jnp.float32) * (16.0 / pillars)
    total = jnp.zeros((set_total, part), jnp.float32)
    for load, pack in zip(loads, packs):
        factors = lax.dot_general(
            load, normals, (((1,), (1,)), ((), ())), preferred_element_type=jnp.float32
        )
        yields = pack[:, set_total : set_total + 1]
        discount = jnp.exp(-tenors[:, None] * (yields + 0.02 * factors)).astype(jnp.bfloat16)
        flow = pack[:, :set_total]
        high = lax.reduce_precision(flow, 8, 7)
        for term in (high, flow - high):
            total = total + lax.dot_general(
                term.astype(jnp.bfloat16),
                discount,
                (((0,), (0,)), ((), ())),
                preferred_element_type=jnp.float32,
            )
    sent = lax.all_to_all(total.astype(jnp.bfloat16), TRADE, 0, 0, tiled=True)
    terms = sent.reshape(quarters, groups // quarters, owned, part).astype(jnp.float32)
    net_value = jnp.sum(terms, axis=1).transpose(1, 0, 2).reshape(owned, scen_rows)

    spread = vol[:, None]
    dist_now = dist_prev + (0.03 - 0.5 * spread * spread) + spread * shock
    crossing = jnp.exp(
        -2.0 * jnp.maximum(dist_prev, 0.0) * jnp.maximum(dist_now, 0.0) / (spread * spread)
    )
    losses = jnp.sum(jnp.maximum(net_value, 0.0) * crossing, axis=1)
    summed = jnp.sum(everywhere(losses, "scen").reshape(-1, owned), axis=0)
    expected_loss = summed / (scen_rows * lax.axis_size("scen"))
    return (net_value, expected_loss)


def solution(mesh):
    chips = Mesh(mesh.devices.reshape(4, 8, 2, 8), ("x", "y", "core", "scen"))
    in_specs = (
        P("scen", TRADE, None),
        P(TRADE, None),
        P(TRADE),
        P(None, TRADE),
        P(TRADE),
        P(TRADE),
        P(TRADE, "scen"),
        P(TRADE, "scen"),
        P(TRADE),
    )
    out_specs = (P(TRADE, "scen"), P(TRADE))
    return jax.shard_map(body, mesh=chips, in_specs=in_specs, out_specs=out_specs, check_vma=False)
```

time: 331 us -> 106 us (0.32)
  waiting for transfers between devices: 286 us -> 40.3 us
  starting transfers between devices: 0.08 us -> 35.4 us
  between operations: 14.8 us -> 1.59 us
    psum x1 -> x0, waiting for transfers between devices: 198 us -> none  [body(): whole = lax.psum(partial_value, 'trade')]
    all_gather x1 -> x0, waiting for transfers between devices: 87.7 us -> none  [body(): lax.all_gather(draws, 'trade', axis=1, tiled=True)[0]]
    all_to_all x0 -> x2, waiting for transfers between devices: none -> 22.6 us  [the longest x1 11.5 us: body(): sent = lax.all_to_all(total.astype(jnp.bfloat16), TRADE, 0, 0, tiled=True)]
    ppermute x0 -> x7, starting transfers between devices: none -> 20.6 us  [shift(): lax.ppermute(value, axis, [(i, (i + by) % size) for i in range(size)])]
    psum x1 -> x0, blocking collectives: 18.1 us -> none  [body(): summed = lax.psum(jnp.sum(losses, axis=1), 'scen')]
    all_to_all x0 -> x1, blocking collectives: none -> 17.8 us  [everywhere(): return lax.all_to_all(copies, axis, 0, 0, tiled=True)]
    ppermute x0 -> x7, waiting for transfers between devices: none -> 17.7 us  [shift(): lax.ppermute(value, axis, [(i, (i + by) % size) for i in range(size)])]
    all_to_all x0 -> x2, starting transfers between devices: none -> 14.7 us  [the longest x1 7.64 us: body(): sent = lax.all_to_all(total.astype(jnp.bfloat16), TRADE, 0, 0, tiled=True)]
  transfers between devices with their start and end apart: 2 -> 9, of which waited for: 2 -> 5; matrix products, arithmetic and copies ran while one was open for 1% -> 6% of each run, Pallas kernels for 0% -> 0%
where the time goes in v1:
time: 106 us
  waiting for transfers between devices  40.3 us (38%)
  starting transfers between devices  35.4 us (33%)
  blocking collectives  17.8 us (17%)
  matrix products  6.5 us (6%)
  other arithmetic  2.15 us (2%)
  local copies, waits for them, and re-layouts  2.14 us (2%)
  between operations  1.59 us (2%)
    ppermute x7, starting transfers between devices, shift(): lax.ppermute(value, axis, [(i, (i + by) % size) for i in range(size)])  20.6 us
    all_to_all x1, blocking collectives, everywhere(): return lax.all_to_all(copies, axis, 0, 0, tiled=True)  17.8 us
    ppermute x7, waiting for transfers between devices, shift(): lax.ppermute(value, axis, [(i, (i + by) % size) for i in range(size)])  17.7 us
    all_to_all x1, waiting for transfers between devices, body(): sent = lax.all_to_all(total.astype(jnp.bfloat16), TRADE, 0, 0, tiled=True)  11.5 us
    all_to_all x1, waiting for transfers between devices, everywhere(): return lax.all_to_all(copies, axis, 0, 0, tiled=True)  11 us
    all_to_all x1, starting transfers between devices, body(): sent = lax.all_to_all(total.astype(jnp.bfloat16), TRADE, 0, 0, tiled=True)  7.64 us
    all_to_all x1, starting transfers between devices, everywhere(): return lax.all_to_all(copies, axis, 0, 0, tiled=True)  7.1 us
    dot_general x8, matrix products, body(): lax.dot_general(term.astype(jnp.bfloat16), discount, (((0,), (0,)), ((),...  2.87 us
  transfers between devices with their start and end apart: 9, of which 5 were waited for; matrix products, arithmetic and copies ran while one was open for 6% of the time, Pallas kernels for 0%

profile of v1, /device:TPU:6, one launch (start us, length us, event | category | flops | bytes accessed | tf_op | source)
XLA Modules:
  0.0 105.8 jit_solution(16359723019025572454)
XLA Ops:
  0.6 0.0 copy-start
  0.6 0.0 copy-start.6
  0.7 1.7 %broadcast_in_dim.17 = bf16[8,8,4096]{2,1,0:T(8,128)(2,1)} broadcast(bf16[8,4096]{1,0:T(8,128)(2,1)} %bitcast.43), dimensions={1,2} | broadcast | bytes 589824 | tf_op jit(solution)/shard_map/broadcast_in_dim | solution.py:16
  2.4 7.1 %all-to-all-start = ((bf16[8,8,4096]{2,1,0:T(8,128)(2,1)}), bf16[8,8,4096]{2,1,0:T(8,128)(2,1)S(1)}, u32[]{:S(2)}, u32[]{:S(2)}) async-start(bf16[8,8,4096]{2,1,0:T(8,128)(2,1)} %broadcast_in_dim.17), calls=%async_computation | async-start | bytes 1048576 | tf_op jit(solution)/shard_map/all_to_all | solution.py:17
  10.1 0.0 copy-done
  10.1 0.0 copy-done.6
  10.1 0.0 copy-start.4
  10.2 0.0 copy-start.1
  10.2 1.6 %fusion.9 = f32[64,1024]{1,0:T(8,128)S(1)} fusion(bf16[64,2048]{1,0:T(8,128)(2,1)S(1)} %copy-done, s32[2048]{0:T(1024)S(1)} %copy-done.6, pred[2048]{0:T(1024)(128)(4,1)S(1)} %iota_compare_fusion.1), kind=kOutput, calls=%fused_computation.13 | convolution fusion | flops 276824064 | bytes 534528 | tf_op jit(solution)/shard_map/dot_general | solution.py:27
  11.8 0.0 copy-done.4
  11.8 0.1 add.97
  11.9 0.7 pad_maximum_fusion
  12.6 3.3 %collective-permute-start.5 = (f32[64,1152]{1,0:T(8,128)}, f32[64,1152]{1,0:T(8,128)S(1)}, u32[]{:S(2)}, u32[]{:S(2)}) collective-permute-start(f32[64,1152]{1,0:T(8,128)} %pad_maximum_fusion), channel_id=1, source_target_pairs={{0,256},{128,384},{256,0},{384,128},{1,257},{129,385},{257,1},{385... | collective-permute-start | bytes 884744 | tf_op jit(solution)/shard_map/ppermute | solution.py:11
  15.9 11.0 %all-to-all-done = bf16[8,8,4096]{2,1,0:T(8,128)(2,1)S(1)} async-done(((bf16[8,8,4096]{2,1,0:T(8,128)(2,1)}), bf16[8,8,4096]{2,1,0:T(8,128)(2,1)S(1)}, u32[]{:S(2)}, u32[]{:S(2)}) %all-to-all-start) | async-done | bytes 524320 | tf_op jit(solution)/shard_map/all_to_all | solution.py:17
  27.0 1.9 %collective-permute-start = (bf16[8,8,4096]{2,1,0:T(8,128)(2,1)S(1)}, bf16[8,8,4096]{2,1,0:T(8,128)(2,1)S(1)}, u32[]{:S(2)}, u32[]{:S(2)}) collective-permute-start(bf16[8,8,4096]{2,1,0:T(8,128)(2,1)S(1)} %all-to-all-done), channel_id=1, source_target_pairs={{0,8},{8,0},{1,9},{9,1},{2,10},{10,2},{3,11},{11,3},{4,12},{12,4},... | collective-permute-start | bytes 1572872 | tf_op jit(solution)/shard_map/ppermute | solution.py:11
  28.9 2.7 %collective-permute-start.3 = (f32[64,1152]{1,0:T(8,128)}, f32[64,1152]{1,0:T(8,128)S(1)}, u32[]{:S(2)}, u32[]{:S(2)}) collective-permute-start(f32[64,1152]{1,0:T(8,128)} %pad_maximum_fusion), channel_id=1, source_target_pairs={{0,384},{128,0},{256,128},{384,256},{1,385},{129,1},{257,129},{385... | collective-permute-start | bytes 884744 | tf_op jit(solution)/shard_map/ppermute | solution.py:11
  31.6 4.3 %collective-permute-start.1 = (f32[64,1152]{1,0:T(8,128)}, f32[64,1152]{1,0:T(8,128)S(1)}, u32[]{:S(2)}, u32[]{:S(2)}) collective-permute-start(f32[64,1152]{1,0:T(8,128)} %pad_maximum_fusion), channel_id=1, source_target_pairs={{0,128},{128,256},{256,384},{384,0},{1,129},{129,257},{257,385},{3... | collective-permute-start | bytes 884744 | tf_op jit(solution)/shard_map/ppermute | solution.py:11
  35.9 0.0 copy-done.1
  36.0 2.1 %collective-permute-start.6 = (bf16[64,4096]{1,0:T(8,128)(2,1)S(1)}, bf16[64,4096]{1,0:T(8,128)(2,1)S(1)}, u32[]{:S(2)}, u32[]{:S(2)}) collective-permute-start(bf16[64,4096]{1,0:T(8,128)(2,1)S(1)} %copy-done.1), channel_id=1, source_target_pairs={{0,256},{128,384},{256,0},{384,128},{1,257},{129,385},{257,1},{385... | collective-permute-start | bytes 1572872 | tf_op jit(solution)/shard_map/ppermute | solution.py:11
  38.1 0.0 collective-permute-done.5
  38.1 2.6 %collective-permute-start.4 = (bf16[64,4096]{1,0:T(8,128)(2,1)S(1)}, bf16[64,4096]{1,0:T(8,128)(2,1)S(1)}, u32[]{:S(2)}, u32[]{:S(2)}) collective-permute-start(bf16[64,4096]{1,0:T(8,128)(2,1)S(1)} %copy-done.1), channel_id=1, source_target_pairs={{0,384},{128,0},{256,128},{384,256},{1,385},{129,1},{257,129},{385... | collective-permute-start | bytes 1572872 | tf_op jit(solution)/shard_map/ppermute | solution.py:11
  40.7 0.1 slice_reduce_fusion
  40.8 0.8 collective-permute-done.3
  41.6 3.7 %collective-permute-start.2 = (bf16[64,4096]{1,0:T(8,128)(2,1)S(1)}, bf16[64,4096]{1,0:T(8,128)(2,1)S(1)}, u32[]{:S(2)}, u32[]{:S(2)}) collective-permute-start(bf16[64,4096]{1,0:T(8,128)(2,1)S(1)} %copy-done.1), channel_id=1, source_target_pairs={{0,128},{128,256},{256,384},{384,0},{1,129},{129,257},{257,385},{3... | collective-permute-start | bytes 1572872 | tf_op jit(solution)/shard_map/ppermute | solution.py:11
  45.3 0.1 slice_reduce_fusion.1
  45.4 9.3 %collective-permute-done.1 = f32[64,1152]{1,0:T(8,128)S(1)} collective-permute-done((f32[64,1152]{1,0:T(8,128)}, f32[64,1152]{1,0:T(8,128)S(1)}, u32[]{:S(2)}, u32[]{:S(2)}) %collective-permute-start.1) | collective-permute-done | bytes 294944 | tf_op jit(solution)/shard_map/ppermute | solution.py:11
  54.7 0.1 slice_reduce_fusion.2
  54.8 0.0 collective-permute-done
  54.8 0.1 maximum_select_fusion
  54.9 0.5 fusion.13
  55.4 0.0 collective-permute-done.6
  55.4 0.5 exponential_convert_fusion
  56.0 0.3 fusion.25
  56.2 0.3 fusion.18
  56.5 0.3 fusion.27
  56.8 7.6 %collective-permute-done.4 = bf16[64,4096]{1,0:T(8,128)(2,1)S(1)} collective-permute-done((bf16[64,4096]{1,0:T(8,128)(2,1)S(1)}, bf16[64,4096]{1,0:T(8,128)(2,1)S(1)}, u32[]{:S(2)}, u32[]{:S(2)}) %collective-permute-start.4) | collective-permute-done | bytes 524320 | tf_op jit(solution)/shard_map/ppermute | solution.py:11
  64.4 0.5 exponential_convert_fusion.1
  64.8 0.3 fusion.20
  65.1 0.3 fusion.26
  65.4 0.3 convolution_add_fusion.1
  65.7 0.0 collective-permute-done.2
  65.7 0.5 exponential_convert_fusion.2
  66.2 0.3 fusion.22
  66.4 0.0 copy-start.5
  66.4 0.0 copy-start.2
  66.5 0.0 copy-start.3
  66.5 1.0 fusion.8
  67.5 7.6 %all-to-all-start.1 = ((bf16[64,16,128]{2,1,0:T(8,128)(2,1)}), bf16[64,16,128]{2,1,0:T(8,128)(2,1)S(1)}, u32[]{:S(2)}, u32[]{:S(2)}) async-start(bf16[64,16,128]{2,1,0:T(8,128)(2,1)} %bitcast.6), calls=%async_computation.1 | async-start | bytes 524288 | tf_op jit(solution)/shard_map/all_to_all | solution.py:72
  75.1 0.0 copy-done.5
  75.2 11.5 %all-to-all-done.1 = bf16[64,16,128]{2,1,0:T(8,128)(2,1)S(1)} async-done(((bf16[64,16,128]{2,1,0:T(8,128)(2,1)}), bf16[64,16,128]{2,1,0:T(8,128)(2,1)S(1)}, u32[]{:S(2)}, u32[]{:S(2)}) %all-to-all-start.1) | async-done | bytes 262176 | tf_op jit(solution)/shard_map/all_to_all | solution.py:72
  86.7 0.0 copy-done.2
  86.7 0.0 copy-done.3
  86.8 0.7 multiply_reduce_fusion
  87.5 17.8 %all_to_all.20 = f32[8,1,16]{2,1,0:T(1,128)S(1)} all-to-all(f32[8,1,16]{2,1,0:T(1,128)S(1)} %broadcast_in_dim.18), channel_id=1, replica_groups=mesh['x'=4,'y'=8,'core'=2,'scen'=8] {'scen'}, dimensions={0} | all-to-all | bytes 1024 | tf_op jit(solution)/shard_map/all_to_all | solution.py:17
  105.3 0.5 broadcast_multiply_fusion
  (6 shorter events, 0.1 us)
Async XLA Ops:
  0.6 9.5 %copy-start = (bf16[64,2048]{1,0:T(8,128)(2,1)S(1)}, bf16[64,2048]{1,0:T(8,128)(2,1)}, u32[]{:S(2)}) copy-start(bf16[64,2048]{1,0:T(8,128)(2,1)} %param.12) | copy-start | bytes 786436
  0.6 9.5 %copy-start.6 = (s32[2048]{0:T(1024)S(1)}, s32[2048]{0:T(1024)}, u32[]{:S(2)}) copy-start(s32[2048]{0:T(1024)} %param.13) | copy-start | bytes 24580
  2.4 24.6 %all-to-all-start = ((bf16[8,8,4096]{2,1,0:T(8,128)(2,1)}), bf16[8,8,4096]{2,1,0:T(8,128)(2,1)S(1)}, u32[]{:S(2)}, u32[]{:S(2)}) async-start(bf16[8,8,4096]{2,1,0:T(8,128)(2,1)} %broadcast_in_dim.17), calls=%async_computation | async-start | bytes 1048576 | tf_op jit(solution)/shard_map/all_to_all | solution.py:17
  10.1 1.6 %copy-start.4 = (f32[64]{0:T(128)S(1)}, f32[64]{0:T(128)}, u32[]{:S(2)}) copy-start(f32[64]{0:T(128)} %param.11) | copy-start | bytes 772
  10.2 25.8 %copy-start.1 = (bf16[64,4096]{1,0:T(8,128)(2,1)S(1)}, bf16[64,4096]{1,0:T(8,128)(2,1)}, u32[]{:S(2)}) copy-start(bf16[64,4096]{1,0:T(8,128)(2,1)} %param.10) | copy-start | bytes 1572868
  12.6 25.5 %collective-permute-start.5 = (f32[64,1152]{1,0:T(8,128)}, f32[64,1152]{1,0:T(8,128)S(1)}, u32[]{:S(2)}, u32[]{:S(2)}) collective-permute-start(f32[64,1152]{1,0:T(8,128)} %pad_maximum_fusion), channel_id=1, source_target_pairs={{0,256},{128,384},{256,0},{384,128},{1,257},{129,385},{257,1},{385... | collective-permute-start | bytes 884744 | tf_op jit(solution)/shard_map/ppermute | solution.py:11
  27.0 27.8 %collective-permute-start = (bf16[8,8,4096]{2,1,0:T(8,128)(2,1)S(1)}, bf16[8,8,4096]{2,1,0:T(8,128)(2,1)S(1)}, u32[]{:S(2)}, u32[]{:S(2)}) collective-permute-start(bf16[8,8,4096]{2,1,0:T(8,128)(2,1)S(1)} %all-to-all-done), channel_id=1, source_target_pairs={{0,8},{8,0},{1,9},{9,1},{2,10},{10,2},{3,11},{11,3},{4,12},{12,4},... | collective-permute-start | bytes 1572872 | tf_op jit(solution)/shard_map/ppermute | solution.py:11
  28.9 12.7 %collective-permute-start.3 = (f32[64,1152]{1,0:T(8,128)}, f32[64,1152]{1,0:T(8,128)S(1)}, u32[]{:S(2)}, u32[]{:S(2)}) collective-permute-start(f32[64,1152]{1,0:T(8,128)} %pad_maximum_fusion), channel_id=1, source_target_pairs={{0,384},{128,0},{256,128},{384,256},{1,385},{129,1},{257,129},{385... | collective-permute-start | bytes 884744 | tf_op jit(solution)/shard_map/ppermute | solution.py:11
  31.6 23.1 %collective-permute-start.1 = (f32[64,1152]{1,0:T(8,128)}, f32[64,1152]{1,0:T(8,128)S(1)}, u32[]{:S(2)}, u32[]{:S(2)}) collective-permute-start(f32[64,1152]{1,0:T(8,128)} %pad_maximum_fusion), channel_id=1, source_target_pairs={{0,128},{128,256},{256,384},{384,0},{1,129},{129,257},{257,385},{3... | collective-permute-start | bytes 884744 | tf_op jit(solution)/shard_map/ppermute | solution.py:11
  36.0 19.5 %collective-permute-start.6 = (bf16[64,4096]{1,0:T(8,128)(2,1)S(1)}, bf16[64,4096]{1,0:T(8,128)(2,1)S(1)}, u32[]{:S(2)}, u32[]{:S(2)}) collective-permute-start(bf16[64,4096]{1,0:T(8,128)(2,1)S(1)} %copy-done.1), channel_id=1, source_target_pairs={{0,256},{128,384},{256,0},{384,128},{1,257},{129,385},{257,1},{385... | collective-permute-start | bytes 1572872 | tf_op jit(solution)/shard_map/ppermute | solution.py:11
  38.1 26.3 %collective-permute-start.4 = (bf16[64,4096]{1,0:T(8,128)(2,1)S(1)}, bf16[64,4096]{1,0:T(8,128)(2,1)S(1)}, u32[]{:S(2)}, u32[]{:S(2)}) collective-permute-start(bf16[64,4096]{1,0:T(8,128)(2,1)S(1)} %copy-done.1), channel_id=1, source_target_pairs={{0,384},{128,0},{256,128},{384,256},{1,385},{129,1},{257,129},{385... | collective-permute-start | bytes 1572872 | tf_op jit(solution)/shard_map/ppermute | solution.py:11
  41.6 24.1 %collective-permute-start.2 = (bf16[64,4096]{1,0:T(8,128)(2,1)S(1)}, bf16[64,4096]{1,0:T(8,128)(2,1)S(1)}, u32[]{:S(2)}, u32[]{:S(2)}) collective-permute-start(bf16[64,4096]{1,0:T(8,128)(2,1)S(1)} %copy-done.1), channel_id=1, source_target_pairs={{0,128},{128,256},{256,384},{384,0},{1,129},{129,257},{257,385},{3... | collective-permute-start | bytes 1572872 | tf_op jit(solution)/shard_map/ppermute | solution.py:11
  66.4 8.7 %copy-start.5 = (f32[16]{0:T(128)S(1)}, f32[16]{0:T(128)}, u32[]{:S(2)}) copy-start(f32[16]{0:T(128)} %param.17) | copy-start | bytes 196
  66.4 20.3 %copy-start.2 = (f32[16,512]{1,0:T(8,128)S(1)}, f32[16,512]{1,0:T(8,128)}, u32[]{:S(2)}) copy-start(f32[16,512]{1,0:T(8,128)} %param.16) | copy-start | bytes 98308
  66.5 20.3 %copy-start.3 = (f32[16,512]{1,0:T(8,128)S(1)}, f32[16,512]{1,0:T(8,128)}, u32[]{:S(2)}) copy-start(f32[16,512]{1,0:T(8,128)} %param.15) | copy-start | bytes 98308
  67.5 19.2 %all-to-all-start.1 = ((bf16[64,16,128]{2,1,0:T(8,128)(2,1)}), bf16[64,16,128]{2,1,0:T(8,128)(2,1)S(1)}, u32[]{:S(2)}, u32[]{:S(2)}) async-start(bf16[64,16,128]{2,1,0:T(8,128)(2,1)} %bitcast.6), calls=%async_computation.1 | async-start | bytes 524288 | tf_op jit(solution)/shard_map/all_to_all | solution.py:72

commit v2 on v1

v2 whole, which is shorter than its diff:
```python
import jax
import jax.numpy as jnp
from jax import lax
from jax.experimental import pallas as pl
from jax.experimental.pallas import tpu as pltpu
from jax.sharding import Mesh, PartitionSpec as P

LANES = 128
LIMIT = 16
HINT = 5 * 10**9
PACK_LIMIT = 62
TRADE = ("x", "y", "core")


def shift(value, axis, by):
    size = lax.axis_size(axis)
    return lax.ppermute(value, axis, [(i, (i + by) % size) for i in range(size)])


def everywhere(value, axis):
    size = lax.axis_size(axis)
    copies = jnp.broadcast_to(value[None], (size, *value.shape))
    return lax.all_to_all(copies, axis, 0, 0, tiled=True)


def pack_kernel(
    live_ref, cash_hbm, id_ref, yield_ref, load_hbm, draw_hbm, out_hbm, copies_hbm,
    cash_ref, load_ref, draw_ref, fold_ref, sems
):
    pillars, trades = cash_ref.shape
    width = load_hbm.shape[1]
    rows = fold_ref.shape[0]
    set_total = width * rows // pillars
    cash_in = pltpu.make_async_copy(cash_hbm, cash_ref, sems.at[0])
    cash_in.start()
    draw_in = pltpu.make_async_copy(draw_hbm.at[0], draw_ref, sems.at[1])
    draw_in.start()
    load_in = pltpu.make_async_copy(load_hbm, load_ref.at[:, pl.ds(0, width)], sems.at[2])
    load_in.start()
    diagonal = lax.broadcasted_iota(jnp.int32, (pillars, pillars), 0) == lax.broadcasted_iota(
        jnp.int32, (pillars, pillars), 1
    )
    level = jnp.sum(jnp.where(diagonal, yield_ref[...], 0.0), axis=1, keepdims=True)
    upper = level.astype(jnp.bfloat16).astype(jnp.float32)
    middle = (level - upper).astype(jnp.bfloat16).astype(jnp.float32)
    lower = level - upper - middle
    lane = lax.broadcasted_iota(jnp.int32, (pillars, LANES), 1)
    terms = jnp.where(
        lane == 0, upper, jnp.where(lane == 1, middle, jnp.where(lane == 2, lower, 0.0))
    )
    load_ref[:, width:] = terms.astype(jnp.bfloat16)
    alive = lax.broadcasted_iota(jnp.int32, (1, trades), 1) < live_ref[0]
    owner = jnp.where(alive, id_ref[...], -1)
    fold_ref[:, width:] = jnp.zeros((rows, LANES), jnp.bfloat16)
    draw_in.wait()
    moves = [
        pltpu.make_async_copy(draw_ref, copies_hbm.at[i], sems.at[5 + i])
        for i in range(copies_hbm.shape[0])
    ]
    for move in moves:
        move.start()
    cash_in.wait()
    load_in.wait()
    load_out = pltpu.make_async_copy(load_ref, out_hbm.at[pl.ds(0, pillars)], sems.at[3])
    load_out.start()
    for first in range(0, set_total, 256):
        numbers = first + lax.broadcasted_iota(jnp.int32, (256, trades), 0)
        member = jnp.where(numbers == owner, 1.0, 0.0).astype(jnp.bfloat16)
        flows = lax.dot_general(
            cash_ref[...], member, (((1,), (1,)), ((), ())), preferred_element_type=jnp.float32
        ).astype(jnp.bfloat16)
        for i in range(pillars // rows):
            fold_ref[:, i * set_total + first : i * set_total + first + 256] = flows[
                i * rows : (i + 1) * rows
            ]
    fold_out = pltpu.make_async_copy(fold_ref, out_hbm.at[pl.ds(pillars, rows)], sems.at[4])
    fold_out.start()
    load_out.wait()
    fold_out.wait()
    for move in moves:
        move.wait()


def unfold_kernel(pack_ref, out_ref):
    pillars, set_total = out_ref.shape
    rows = pack_ref.shape[0] - pillars
    for i in range(pillars // rows):
        out_ref[i * rows : (i + 1) * rows, :] = pack_ref[
            pillars:, i * set_total : (i + 1) * set_total
        ]


def discounts(pack_ref, pillars, normals_ref):
    width = normals_ref.shape[1]
    factors = lax.dot_general(
        pack_ref[:pillars, :width],
        normals_ref[...],
        (((1,), (1,)), ((), ())),
        preferred_element_type=jnp.float32,
    )
    step = (lax.broadcasted_iota(jnp.int32, (pillars, 1), 0) + 1).astype(jnp.float32)
    level = jnp.sum(pack_ref[:pillars, width:].astype(jnp.float32), axis=1, keepdims=True)
    return jnp.exp(-step * (16.0 / pillars) * (level + 0.02 * factors)).astype(jnp.bfloat16)


def unfold(pack_ref, pillars, set_total):
    rows = pack_ref.shape[0] - pillars
    return jnp.concatenate(
        [
            pack_ref[pillars:, i * set_total : (i + 1) * set_total]
            for i in range(pillars // rows)
        ],
        axis=0,
    )


def first_kernel(
    core_ref, mine_ref, other_ref, own_ref, far_ref, early_ref, normals_ref, discount_ref, flow_ref
):
    pillars = early_ref.shape[0]
    set_total = early_ref.shape[1]
    rows = mine_ref.shape[1]

    def place(even_ref, odd_ref):
        for i in range(mine_ref.shape[0]):
            normals_ref[2 * i * rows : 2 * (i + 1) * rows, :] = jnp.concatenate(
                [even_ref[i], odd_ref[i]], axis=0
            )

    @pl.when(core_ref[0] == 0)
    def _():
        place(mine_ref, other_ref)

    @pl.when(core_ref[0] != 0)
    def _():
        place(other_ref, mine_ref)

    discount_ref[:pillars, :] = discounts(own_ref, pillars, normals_ref)
    discount_ref[pillars:, :] = discounts(far_ref, pillars, normals_ref)
    flow_ref[:pillars, :] = unfold(own_ref, pillars, set_total)
    flow_ref[pillars:, :] = early_ref[...]


def price_kernel(normals_ref, discount_ref, flow_ref, *refs):
    pack_refs, out_ref = refs[:-1], refs[-1]
    pillars = discount_ref.shape[0] // 2
    set_total = out_ref.shape[0]
    prices = [discount_ref[...]] + [discounts(ref, pillars, normals_ref) for ref in pack_refs]
    flows = [flow_ref[...]] + [unfold(ref, pillars, set_total) for ref in pack_refs]
    out_ref[...] = lax.dot_general(
        jnp.concatenate(flows, axis=0),
        jnp.concatenate(prices, axis=0),
        (((0,), (0,)), ((), ())),
        preferred_element_type=jnp.float32,
    ).astype(jnp.bfloat16)


def body(draws, loadings, base_yield, cashflows, netting_id, live_trades, dist_prev, shock, vol):
    pillars = loadings.shape[0]
    owned, scen_rows = dist_prev.shape
    quarters = lax.axis_size("x")
    groups = quarters * lax.axis_size("y") * lax.axis_size("core")
    set_total = owned * groups
    part = scen_rows // quarters
    width = loadings.shape[1]
    rows = pillars * set_total // width
    vmem = pl.BlockSpec(memory_space=pltpu.VMEM)
    hbm = pl.BlockSpec(memory_space=pltpu.HBM)
    smem = pl.BlockSpec(memory_space=pltpu.SMEM)
    params = pltpu.CompilerParams(vmem_limit_bytes=LIMIT << 20)

    packed, copies = pl.pallas_call(
        pack_kernel,
        out_shape=(
            jax.ShapeDtypeStruct((pillars + rows, width + LANES), jnp.bfloat16),
            jax.ShapeDtypeStruct((lax.axis_size("y"), *draws.shape[1:]), jnp.bfloat16),
        ),
        in_specs=[smem, hbm, vmem, vmem, hbm, hbm],
        out_specs=(hbm, hbm),
        scratch_shapes=[
            pltpu.VMEM(cashflows.shape, jnp.bfloat16),
            pltpu.VMEM((pillars, width + LANES), jnp.bfloat16),
            pltpu.VMEM(draws.shape[1:], jnp.bfloat16),
            pltpu.VMEM((rows, width + LANES), jnp.bfloat16),
            pltpu.SemaphoreType.DMA((5 + lax.axis_size("y"),)),
        ],
        compiler_params=pltpu.CompilerParams(vmem_limit_bytes=PACK_LIMIT << 20),
        name="pack",
    )(live_trades, cashflows, netting_id[None, :], base_yield[None, :], loadings, draws)
    packs = [shift(packed, "x", by) for by in (2, 1, -1)]
    mine = lax.all_to_all(copies, "y", 0, 0, tiled=True)
    early = pl.pallas_call(
        unfold_kernel,
        out_shape=jax.ShapeDtypeStruct((pillars, set_total), jnp.bfloat16),
        in_specs=[vmem],
        out_specs=vmem,
        compiler_params=params,
        cost_estimate=pl.CostEstimate(flops=HINT, bytes_accessed=0, transcendentals=0),
        name="unfold",
    )(packs[0])
    mine, early = lax.optimization_barrier((mine, early))
    other = shift(mine, "core", 1)
    normals, discount, flow = pl.pallas_call(
        first_kernel,
        out_shape=(
            jax.ShapeDtypeStruct((part, width), jnp.bfloat16),
            jax.ShapeDtypeStruct((2 * pillars, part), jnp.bfloat16),
            jax.ShapeDtypeStruct((2 * pillars, set_total), jnp.bfloat16),
        ),
        in_specs=[smem, vmem, vmem, vmem, vmem, vmem],
        out_specs=(vmem, vmem, vmem),
        compiler_params=params,
        name="first",
    )(lax.axis_index("core").astype(jnp.int32)[None], mine, other, packed, packs[0], early)
    total = pl.pallas_call(
        price_kernel,
        out_shape=jax.ShapeDtypeStruct((set_total, part), jnp.bfloat16),
        in_specs=[vmem] * 5,
        out_specs=vmem,
        compiler_params=params,
        name="price",
    )(normals, discount, flow, *packs[1:])
    sent = lax.all_to_all(total, TRADE, 0, 0, tiled=True)
    terms = sent.reshape(quarters, groups // quarters, owned, part).astype(jnp.float32)
    net_value = jnp.sum(terms, axis=1).transpose(1, 0, 2).reshape(owned, scen_rows)

    spread = vol[:, None]
    dist_now = dist_prev + (0.03 - 0.5 * spread * spread) + spread * shock
    crossing = jnp.exp(
        -2.0 * jnp.maximum(dist_prev, 0.0) * jnp.maximum(dist_now, 0.0) / (spread * spread)
    )
    losses = jnp.sum(jnp.maximum(net_value, 0.0) * crossing, axis=1)
    tile = jnp.broadcast_to(jnp.pad(losses, (0, LANES - owned)), (8, LANES))
    summed = jnp.sum(everywhere(tile, "scen").reshape(-1, 8, LANES)[:, 0, :owned], axis=0)
    expected_loss = summed / (scen_rows * lax.axis_size("scen"))
    return (net_value, expected_loss)


def solution(mesh):
    chips = Mesh(mesh.devices.reshape(4, 8, 2, 8), ("x", "y", "core", "scen"))
    in_specs = (
        P("scen", TRADE, None),
        P(TRADE, None),
        P(TRADE),
        P(None, TRADE),
        P(TRADE),
        P(TRADE),
        P(TRADE, "scen"),
        P(TRADE, "scen"),
        P(TRADE),
    )
    out_specs = (P(TRADE, "scen"), P(TRADE))
    return jax.shard_map(body, mesh=chips, in_specs=in_specs, out_specs=out_specs, check_vma=False)
```

time: 106 us -> 84.8 us (0.80)
  waiting for transfers between devices: 40.3 us -> 26.1 us
  Pallas kernels: 0 us -> 7.89 us
  matrix products: 6.5 us -> 0 us
  starting transfers between devices: 35.4 us -> 29.3 us
  local copies, waits for them, and re-layouts: 2.14 us -> 0.04 us
    ppermute x7 -> x4, starting transfers between devices: 20.6 us -> 11.3 us  [shift(): lax.ppermute(value, axis, [(i, (i + by) % size) for i in range(size)])]
    ppermute x7 -> x4, waiting for transfers between devices: 17.7 us -> 8.66 us  [shift(): lax.ppermute(value, axis, [(i, (i + by) % size) for i in range(size)])]
    pallas_call x0 -> x4, Pallas kernels: none -> 7.89 us  [the longest x1 4.02 us: body(): pl.pallas_call(pack_kernel, out_shape=(jax.ShapeDtypeStruct((pillars + ro...]
    dot_general x13 -> x0, matrix products: 6.5 us -> none  [the longest x8 2.87 us: body(): lax.dot_general(term.astype(jnp.bfloat16), discount, (((0,), (0,)), ((),...]
    all_to_all x2, waiting for transfers between devices: 22.6 us -> 17.5 us  [the longest x1 11.5 us: body(): sent = lax.all_to_all(total, TRADE, 0, 0, tiled=True)]
    all_to_all x2, starting transfers between devices: 14.7 us -> 18 us  [the longest x1 10.9 us: body(): sent = lax.all_to_all(total, TRADE, 0, 0, tiled=True)]
    broadcast_in_dim x2 -> x0, local copies, waits for them, and re-layouts: 1.71 us -> none  [everywhere(): copies = jnp.broadcast_to(value[None], (size, *value.shape))]
  transfers between devices with their start and end apart: 9 -> 6, of which waited for: 5 -> 5; matrix products, arithmetic and copies ran while one was open for 6% -> 0% of each run, Pallas kernels for 0% -> 2%
where the time goes in v2:
time: 84.8 us; the launch traced here: 84.3 us
  starting transfers between devices  29.3 us (35%)
  waiting for transfers between devices  26.1 us (31%)
  blocking collectives  18.1 us (21%)
  Pallas kernels  7.89 us (9%)
  between operations  1.42 us (2%)
  other arithmetic  1.31 us (2%)
    all_to_all x1, blocking collectives, everywhere(): return lax.all_to_all(copies, axis, 0, 0, tiled=True)  18.1 us
    all_to_all x1, waiting for transfers between devices, body(): sent = lax.all_to_all(total, TRADE, 0, 0, tiled=True)  11.5 us
    ppermute x4, starting transfers between devices, shift(): lax.ppermute(value, axis, [(i, (i + by) % size) for i in range(size)])  11.3 us
    all_to_all x1, starting transfers between devices, body(): sent = lax.all_to_all(total, TRADE, 0, 0, tiled=True)  10.9 us
    ppermute x4, waiting for transfers between devices, shift(): lax.ppermute(value, axis, [(i, (i + by) % size) for i in range(size)])  8.66 us
    all_to_all x1, starting transfers between devices, body(): mine = lax.all_to_all(copies, 'y', 0, 0, tiled=True)  7.11 us
    all_to_all x1, waiting for transfers between devices, body(): mine = lax.all_to_all(copies, 'y', 0, 0, tiled=True)  5.96 us
    pallas_call x1, Pallas kernels, body(): pl.pallas_call(pack_kernel, out_shape=(jax.ShapeDtypeStruct((pillars + ro...  4.02 us
  transfers between devices with their start and end apart: 6, of which 5 were waited for; matrix products, arithmetic and copies ran while one was open for 0% of the time, Pallas kernels for 2%

profile of v2, /device:TPU:6, one launch (start us, length us, event | category | flops | bytes accessed | tf_op | source)
XLA Modules:
  0.0 84.3 jit_solution(65567855179957531)
XLA Ops:
  1.3 4.0 %pack.1 = (bf16[80,4224]{1,0:T(8,128)(2,1)}, bf16[8,8,4096]{2,1,0:T(8,128)(2,1)}) custom-call(s32[1]{0:T(128)S(6)} %copy.18.live_ref, bf16[64,2048]{1,0:T(8,128)(2,1)} %cash_hbm.1, s32[1,2048]{1,0:T(1,128)} %bitcast.16, f32[1,64]{1,0:T(1,128)} %bitcast.17, bf16[64,4096]{1,0:T(8,128)(2,1)} %load_hbm.1, bf16[1,8,4096]{2,1,0:T(8,128)(2,1)} %draw_hbm.1), custom_call_target="tpu_custom_call" | custom-call | tf_op jit(solution)/shard_map/pack/pallas_call | solution.py:172
  5.3 0.0 copy-start
  5.3 3.4 %collective-permute-start = (bf16[80,4224]{1,0:T(8,128)(2,1)}, bf16[80,4224]{1,0:T(8,128)(2,1)S(1)}, u32[]{:S(2)}, u32[]{:S(2)}) collective-permute-start(bf16[80,4224]{1,0:T(8,128)(2,1)} %get-tuple-element.10.own_ref), channel_id=1, source_target_pairs={{0,256},{128,384},{256,0},{384,128},{1,257},{129,385},{257,1},{385... | collective-permute-start | bytes 2027528 | tf_op jit(solution)/shard_map/ppermute | solution.py:17
  8.8 7.1 %all-to-all-start = ((bf16[8,8,4096]{2,1,0:T(8,128)(2,1)}), bf16[8,8,4096]{2,1,0:T(8,128)(2,1)S(1)}, u32[]{:S(2)}, u32[]{:S(2)}) async-start(bf16[8,8,4096]{2,1,0:T(8,128)(2,1)} %get-tuple-element.9), calls=%async_computation | async-start | bytes 1048576 | tf_op jit(solution)/shard_map/all_to_all | solution.py:191
  15.9 0.0 copy-done
  15.9 4.0 %collective-permute-start.2 = (bf16[80,4224]{1,0:T(8,128)(2,1)S(1)}, bf16[80,4224]{1,0:T(8,128)(2,1)S(1)}, u32[]{:S(2)}, u32[]{:S(2)}) collective-permute-start(bf16[80,4224]{1,0:T(8,128)(2,1)S(1)} %copy-done), channel_id=1, source_target_pairs={{0,128},{128,256},{256,384},{384,0},{1,129},{129,257},{257,385},{3... | collective-permute-start | bytes 2027528 | tf_op jit(solution)/shard_map/ppermute | solution.py:17
  19.9 1.9 %collective-permute-start.3 = (bf16[80,4224]{1,0:T(8,128)(2,1)S(1)}, bf16[80,4224]{1,0:T(8,128)(2,1)S(1)}, u32[]{:S(2)}, u32[]{:S(2)}) collective-permute-start(bf16[80,4224]{1,0:T(8,128)(2,1)S(1)} %copy-done), channel_id=1, source_target_pairs={{0,384},{128,0},{256,128},{384,256},{1,385},{129,1},{257,129},{385... | collective-permute-start | bytes 2027528 | tf_op jit(solution)/shard_map/ppermute | solution.py:17
  21.8 5.3 %collective-permute-done.pack_ref.far_ref = bf16[80,4224]{1,0:T(8,128)(2,1)S(1)} collective-permute-done((bf16[80,4224]{1,0:T(8,128)(2,1)}, bf16[80,4224]{1,0:T(8,128)(2,1)S(1)}, u32[]{:S(2)}, u32[]{:S(2)}) %collective-permute-start) | collective-permute-done | bytes 675872 | tf_op jit(solution)/shard_map/ppermute | solution.py:17
  27.1 6.0 %all-to-all-done.mine_ref = bf16[8,8,4096]{2,1,0:T(8,128)(2,1)S(1)} async-done(((bf16[8,8,4096]{2,1,0:T(8,128)(2,1)}), bf16[8,8,4096]{2,1,0:T(8,128)(2,1)S(1)}, u32[]{:S(2)}, u32[]{:S(2)}) %all-to-all-start) | async-done | bytes 524320 | tf_op jit(solution)/shard_map/all_to_all | solution.py:191
  33.1 1.9 %collective-permute-start.1 = (bf16[8,8,4096]{2,1,0:T(8,128)(2,1)S(1)}, bf16[8,8,4096]{2,1,0:T(8,128)(2,1)}, u32[]{:S(2)}, u32[]{:S(2)}) collective-permute-start(bf16[8,8,4096]{2,1,0:T(8,128)(2,1)S(1)} %all-to-all-done.mine_ref), channel_id=1, source_target_pairs={{0,8},{8,0},{1,9},{9,1},{2,10},{10,2},{3,11},{11,3},{4,12},{12,4},... | collective-permute-start | bytes 1572872 | tf_op jit(solution)/shard_map/ppermute | solution.py:17
  35.0 2.0 %collective-permute-done.1.other_ref = bf16[8,8,4096]{2,1,0:T(8,128)(2,1)} collective-permute-done((bf16[8,8,4096]{2,1,0:T(8,128)(2,1)S(1)}, bf16[8,8,4096]{2,1,0:T(8,128)(2,1)}, u32[]{:S(2)}, u32[]{:S(2)}) %collective-permute-start.1) | collective-permute-done | bytes 524320 | tf_op jit(solution)/shard_map/ppermute | solution.py:17
  37.0 2.0 %first.1 = (bf16[128,4096]{1,0:T(8,128)(2,1)S(1)}, bf16[128,128]{1,0:T(8,128)(2,1)S(1)}, bf16[128,1024]{1,0:T(8,128)(2,1)S(1)}) custom-call(s32[1]{0:T(128)} %bitcast.core_ref, bf16[8,8,4096]{2,1,0:T(8,128)(2,1)S(1)} %all-to-all-done.mine_ref, bf16[8,8,4096]{2,1,0:T(8,128)(2,1)} %collective-permute-done.1.other_ref, bf16[80,4224]{1,0:T(8,128)(2,1)S(1)} %copy-done, ...), custom_call_target="tpu_custom_call" | custom-call | tf_op jit(solution)/shard_map/first/pallas_call | solution.py:203
  39.1 0.0 collective-permute-done.2.refs_0_
  39.1 1.4 %collective-permute-done.3.refs_1_ = bf16[80,4224]{1,0:T(8,128)(2,1)S(1)} collective-permute-done((bf16[80,4224]{1,0:T(8,128)(2,1)S(1)}, bf16[80,4224]{1,0:T(8,128)(2,1)S(1)}, u32[]{:S(2)}, u32[]{:S(2)}) %collective-permute-start.3) | collective-permute-done | bytes 675872 | tf_op jit(solution)/shard_map/ppermute | solution.py:17
  40.4 1.8 %price.1 = bf16[1024,128]{1,0:T(8,128)(2,1)} custom-call(bf16[128,4096]{1,0:T(8,128)(2,1)S(1)} %get-tuple-element.13.normals_ref, bf16[128,128]{1,0:T(8,128)(2,1)S(1)} %get-tuple-element.14.discount_ref, bf16[128,1024]{1,0:T(8,128)(2,1)S(1)} %get-tuple-element.15.flow_ref, bf16[80,4224]{1,0:T(8,128)(2,1)S(1)} %collective-permute-done.2.refs_0_, ...), custom_call_target="tpu_custom_call" | custom-call | tf_op jit(solution)/shard_map/price/pallas_call | solution.py:215
  42.3 0.0 copy-start.3
  42.3 10.9 %all-to-all-start.1 = ((bf16[64,16,128]{2,1,0:T(8,128)(2,1)}), bf16[64,16,128]{2,1,0:T(8,128)(2,1)S(1)}, u32[]{:S(2)}, u32[]{:S(2)}) async-start(bf16[64,16,128]{2,1,0:T(8,128)(2,1)} %bitcast.3), calls=%async_computation.1 | async-start | bytes 524288 | tf_op jit(solution)/shard_map/all_to_all | solution.py:223
  53.2 0.0 copy-done.3
  53.2 0.0 copy-start.1
  53.2 0.0 copy-start.2
  53.3 11.5 %all-to-all-done.1 = bf16[64,16,128]{2,1,0:T(8,128)(2,1)S(1)} async-done(((bf16[64,16,128]{2,1,0:T(8,128)(2,1)}), bf16[64,16,128]{2,1,0:T(8,128)(2,1)S(1)}, u32[]{:S(2)}, u32[]{:S(2)}) %all-to-all-start.1) | async-done | bytes 262176 | tf_op jit(solution)/shard_map/all_to_all | solution.py:223
  64.8 0.0 copy-done.1
  64.8 0.0 copy-done.2
  64.8 0.7 multiply_reduce_fusion
  65.6 18.1 %all_to_all.19 = f32[8,8,128]{2,1,0:T(8,128)S(1)} all-to-all(f32[8,8,128]{2,1,0:T(8,128)S(1)} %broadcast_in_dim_broadcast_in_dim_broadcast_in_dim.3), channel_id=1, replica_groups=mesh['x'=4,'y'=8,'core'=2,'scen'=8] {'scen'}, dimensions={0} | all-to-all | bytes 65536 | tf_op jit(solution)/shard_map/all_to_all | solution.py:23
  83.8 0.5 broadcast_multiply_fusion
  (7 shorter events, 0.1 us)
Async XLA Ops:
  5.3 10.6 %copy-start = (bf16[80,4224]{1,0:T(8,128)(2,1)S(1)}, bf16[80,4224]{1,0:T(8,128)(2,1)}, u32[]{:S(2)}) copy-start(bf16[80,4224]{1,0:T(8,128)(2,1)} %get-tuple-element.10.own_ref) | copy-start | bytes 2027524
  5.3 21.8 %collective-permute-start = (bf16[80,4224]{1,0:T(8,128)(2,1)}, bf16[80,4224]{1,0:T(8,128)(2,1)S(1)}, u32[]{:S(2)}, u32[]{:S(2)}) collective-permute-start(bf16[80,4224]{1,0:T(8,128)(2,1)} %get-tuple-element.10.own_ref), channel_id=1, source_target_pairs={{0,256},{128,384},{256,0},{384,128},{1,257},{129,385},{257,1},{385... | collective-permute-start | bytes 2027528 | tf_op jit(solution)/shard_map/ppermute | solution.py:17
  8.8 24.3 %all-to-all-start = ((bf16[8,8,4096]{2,1,0:T(8,128)(2,1)}), bf16[8,8,4096]{2,1,0:T(8,128)(2,1)S(1)}, u32[]{:S(2)}, u32[]{:S(2)}) async-start(bf16[8,8,4096]{2,1,0:T(8,128)(2,1)} %get-tuple-element.9), calls=%async_computation | async-start | bytes 1048576 | tf_op jit(solution)/shard_map/all_to_all | solution.py:191
  15.9 23.2 %collective-permute-start.2 = (bf16[80,4224]{1,0:T(8,128)(2,1)S(1)}, bf16[80,4224]{1,0:T(8,128)(2,1)S(1)}, u32[]{:S(2)}, u32[]{:S(2)}) collective-permute-start(bf16[80,4224]{1,0:T(8,128)(2,1)S(1)} %copy-done), channel_id=1, source_target_pairs={{0,128},{128,256},{256,384},{384,0},{1,129},{129,257},{257,385},{3... | collective-permute-start | bytes 2027528 | tf_op jit(solution)/shard_map/ppermute | solution.py:17
  19.9 20.5 %collective-permute-start.3 = (bf16[80,4224]{1,0:T(8,128)(2,1)S(1)}, bf16[80,4224]{1,0:T(8,128)(2,1)S(1)}, u32[]{:S(2)}, u32[]{:S(2)}) collective-permute-start(bf16[80,4224]{1,0:T(8,128)(2,1)S(1)} %copy-done), channel_id=1, source_target_pairs={{0,384},{128,0},{256,128},{384,256},{1,385},{129,1},{257,129},{385... | collective-permute-start | bytes 2027528 | tf_op jit(solution)/shard_map/ppermute | solution.py:17
  33.1 3.9 %collective-permute-start.1 = (bf16[8,8,4096]{2,1,0:T(8,128)(2,1)S(1)}, bf16[8,8,4096]{2,1,0:T(8,128)(2,1)}, u32[]{:S(2)}, u32[]{:S(2)}) collective-permute-start(bf16[8,8,4096]{2,1,0:T(8,128)(2,1)S(1)} %all-to-all-done.mine_ref), channel_id=1, source_target_pairs={{0,8},{8,0},{1,9},{9,1},{2,10},{10,2},{3,11},{11,3},{4,12},{12,4},... | collective-permute-start | bytes 1572872 | tf_op jit(solution)/shard_map/ppermute | solution.py:17
  42.3 10.9 %copy-start.3 = (f32[16]{0:T(128)S(1)}, f32[16]{0:T(128)}, u32[]{:S(2)}) copy-start(f32[16]{0:T(128)} %param.17) | copy-start | bytes 196
  42.3 22.5 %all-to-all-start.1 = ((bf16[64,16,128]{2,1,0:T(8,128)(2,1)}), bf16[64,16,128]{2,1,0:T(8,128)(2,1)S(1)}, u32[]{:S(2)}, u32[]{:S(2)}) async-start(bf16[64,16,128]{2,1,0:T(8,128)(2,1)} %bitcast.3), calls=%async_computation.1 | async-start | bytes 524288 | tf_op jit(solution)/shard_map/all_to_all | solution.py:223
  53.2 11.6 %copy-start.1 = (f32[16,512]{1,0:T(8,128)S(1)}, f32[16,512]{1,0:T(8,128)}, u32[]{:S(2)}) copy-start(f32[16,512]{1,0:T(8,128)} %param.16) | copy-start | bytes 98308
  53.2 11.6 %copy-start.2 = (f32[16,512]{1,0:T(8,128)S(1)}, f32[16,512]{1,0:T(8,128)}, u32[]{:S(2)}) copy-start(f32[16,512]{1,0:T(8,128)} %param.15) | copy-start | bytes 98308

commit v3 on v2

--- a/solution.py
+++ b/solution.py
@@ -6,8 +6,8 @@
 from jax.sharding import Mesh, PartitionSpec as P
 
 LANES = 128
+HINT = 25 * 10**8
 LIMIT = 16
-HINT = 5 * 10**9
 PACK_LIMIT = 62
 TRADE = ("x", "y", "core")
 
@@ -24,19 +24,24 @@
 
 
 def pack_kernel(
-    live_ref, cash_hbm, id_ref, yield_ref, load_hbm, draw_hbm, out_hbm, copies_hbm,
-    cash_ref, load_ref, draw_ref, fold_ref, sems
+    live_ref, cash_hbm, id_hbm, yield_hbm, load_hbm, draw_hbm, out_hbm, half_hbm, copies_hbm,
+    cash_ref, load_ref, draw_ref, fold_ref, id_ref, yield_ref, sems
 ):
     pillars, trades = cash_ref.shape
     width = load_hbm.shape[1]
     rows = fold_ref.shape[0]
     set_total = width * rows // pillars
+    yield_in = pltpu.make_async_copy(yield_hbm, yield_ref, sems.at[5])
+    yield_in.start()
+    id_in = pltpu.make_async_copy(id_hbm, id_ref, sems.at[6])
+    id_in.start()
     cash_in = pltpu.make_async_copy(cash_hbm, cash_ref, sems.at[0])
     cash_in.start()
     draw_in = pltpu.make_async_copy(draw_hbm.at[0], draw_ref, sems.at[1])
     draw_in.start()
     load_in = pltpu.make_async_copy(load_hbm, load_ref.at[:, pl.ds(0, width)], sems.at[2])
     load_in.start()
+    yield_in.wait()
     diagonal = lax.broadcasted_iota(jnp.int32, (pillars, pillars), 0) == lax.broadcasted_iota(
         jnp.int32, (pillars, pillars), 1
     )
@@ -49,12 +54,13 @@
         lane == 0, upper, jnp.where(lane == 1, middle, jnp.where(lane == 2, lower, 0.0))
     )
     load_ref[:, width:] = terms.astype(jnp.bfloat16)
+    id_in.wait()
     alive = lax.broadcasted_iota(jnp.int32, (1, trades), 1) < live_ref[0]
     owner = jnp.where(alive, id_ref[...], -1)
     fold_ref[:, width:] = jnp.zeros((rows, LANES), jnp.bfloat16)
     draw_in.wait()
     moves = [
-        pltpu.make_async_copy(draw_ref, copies_hbm.at[i], sems.at[5 + i])
+        pltpu.make_async_copy(draw_ref, copies_hbm.at[i], sems.at[9 + i])
         for i in range(copies_hbm.shape[0])
     ]
     for move in moves:
@@ -63,6 +69,12 @@
     load_in.wait()
     load_out = pltpu.make_async_copy(load_ref, out_hbm.at[pl.ds(0, pillars)], sems.at[3])
     load_out.start()
+    start = pl.multiple_of(lax.rem(lax.axis_index("scen"), 2) * (width // 2), LANES)
+    span = half_hbm.shape[1]
+    load_half = pltpu.make_async_copy(
+        load_ref.at[:, pl.ds(start, span)], half_hbm.at[pl.ds(0, pillars)], sems.at[7]
+    )
+    load_half.start()
     for first in range(0, set_total, 256):
         numbers = first + lax.broadcasted_iota(jnp.int32, (256, trades), 0)
         member = jnp.where(numbers == owner, 1.0, 0.0).astype(jnp.bfloat16)
@@ -75,19 +87,16 @@
             ]
     fold_out = pltpu.make_async_copy(fold_ref, out_hbm.at[pl.ds(pillars, rows)], sems.at[4])
     fold_out.start()
+    fold_half = pltpu.make_async_copy(
+        fold_ref.at[:, pl.ds(start, span)], half_hbm.at[pl.ds(pillars, rows)], sems.at[8]
+    )
+    fold_half.start()
+    load_half.wait()
+    fold_half.wait()
     load_out.wait()
     fold_out.wait()
     for move in moves:
         move.wait()
-
-
-def unfold_kernel(pack_ref, out_ref):
-    pillars, set_total = out_ref.shape
-    rows = pack_ref.shape[0] - pillars
-    for i in range(pillars // rows):
-        out_ref[i * rows : (i + 1) * rows, :] = pack_ref[
-            pillars:, i * set_total : (i + 1) * set_total
-        ]
 
 
 def discounts(pack_ref, pillars, normals_ref):
@@ -114,12 +123,38 @@
     )
 
 
-def first_kernel(
-    core_ref, mine_ref, other_ref, own_ref, far_ref, early_ref, normals_ref, discount_ref, flow_ref
-):
-    pillars = early_ref.shape[0]
-    set_total = early_ref.shape[1]
+def join_kernel(near_half, next_half, out_ref):
+    middle = out_ref.shape[1] - near_half.shape[1]
+    even = lax.rem(lax.axis_index("scen"), 2) == 0
+
+    def join(low_ref, high_ref):
+        out_ref[:, :middle] = low_ref[:, :middle]
+        out_ref[:, middle:] = high_ref[...]
+
+    @pl.when(even)
+    def _():
+        join(near_half, next_half)
+
+    @pl.when(jnp.logical_not(even))
+    def _():
+        join(next_half, near_half)
+
+
+def values(pack_refs, pillars, set_total, normals_ref):
+    return lax.dot_general(
+        jnp.concatenate([unfold(ref, pillars, set_total) for ref in pack_refs], axis=0),
+        jnp.concatenate([discounts(ref, pillars, normals_ref) for ref in pack_refs], axis=0),
+        (((0,), (0,)), ((), ())),
+        preferred_element_type=jnp.float32,
+    )
+
+
+def first_kernel(mine_ref, other_ref, own_ref, far_ref, normals_ref, total_ref):
+    set_total = total_ref.shape[0]
+    width = normals_ref.shape[1]
+    pillars = own_ref.shape[0] * width // (width + set_total)
     rows = mine_ref.shape[1]
+    first = lax.axis_index("core") == 0
 
     def place(even_ref, odd_ref):
         for i in range(mine_ref.shape[0]):
@@ -127,32 +162,24 @@
                 [even_ref[i], odd_ref[i]], axis=0
             )
 
-    @pl.when(core_ref[0] == 0)
+    @pl.when(first)
     def _():
         place(mine_ref, other_ref)
 
-    @pl.when(core_ref[0] != 0)
+    @pl.when(jnp.logical_not(first))
     def _():
         place(other_ref, mine_ref)
 
-    discount_ref[:pillars, :] = discounts(own_ref, pillars, normals_ref)
-    discount_ref[pillars:, :] = discounts(far_ref, pillars, normals_ref)
-    flow_ref[:pillars, :] = unfold(own_ref, pillars, set_total)
-    flow_ref[pillars:, :] = early_ref[...]
-
-
-def price_kernel(normals_ref, discount_ref, flow_ref, *refs):
+    total_ref[...] = values([own_ref, far_ref], pillars, set_total, normals_ref)
+
+
+def price_kernel(normals_ref, total_ref, *refs):
     pack_refs, out_ref = refs[:-1], refs[-1]
-    pillars = discount_ref.shape[0] // 2
     set_total = out_ref.shape[0]
-    prices = [discount_ref[...]] + [discounts(ref, pillars, normals_ref) for ref in pack_refs]
-    flows = [flow_ref[...]] + [unfold(ref, pillars, set_total) for ref in pack_refs]
-    out_ref[...] = lax.dot_general(
-        jnp.concatenate(flows, axis=0),
-        jnp.concatenate(prices, axis=0),
-        (((0,), (0,)), ((), ())),
-        preferred_element_type=jnp.float32,
-    ).astype(jnp.bfloat16)
+    width = normals_ref.shape[1]
+    pillars = pack_refs[0].shape[0] * width // (width + set_total)
+    rest = values(pack_refs, pillars, set_total, normals_ref)
+    out_ref[...] = (total_ref[...] + rest).astype(jnp.bfloat16)
 
 
 def body(draws, loadings, base_yield, cashflows, netting_id, live_trades, dist_prev, shock, vol):
@@ -169,57 +196,62 @@
     smem = pl.BlockSpec(memory_space=pltpu.SMEM)
     params = pltpu.CompilerParams(vmem_limit_bytes=LIMIT << 20)
 
-    packed, copies = pl.pallas_call(
+    packed, half, copies = pl.pallas_call(
         pack_kernel,
         out_shape=(
             jax.ShapeDtypeStruct((pillars + rows, width + LANES), jnp.bfloat16),
+            jax.ShapeDtypeStruct((pillars + rows, width // 2 + LANES), jnp.bfloat16),
             jax.ShapeDtypeStruct((lax.axis_size("y"), *draws.shape[1:]), jnp.bfloat16),
         ),
-        in_specs=[smem, hbm, vmem, vmem, hbm, hbm],
-        out_specs=(hbm, hbm),
+        in_specs=[smem, hbm, hbm, hbm, hbm, hbm],
+        out_specs=(hbm, hbm, hbm),
         scratch_shapes=[
             pltpu.VMEM(cashflows.shape, jnp.bfloat16),
             pltpu.VMEM((pillars, width + LANES), jnp.bfloat16),
             pltpu.VMEM(draws.shape[1:], jnp.bfloat16),
             pltpu.VMEM((rows, width + LANES), jnp.bfloat16),
-            pltpu.SemaphoreType.DMA((5 + lax.axis_size("y"),)),
+            pltpu.VMEM((1, netting_id.shape[0]), jnp.int32),
+            pltpu.VMEM((1, pillars), jnp.float32),
+            pltpu.SemaphoreType.DMA((9 + lax.axis_size("y"),)),
         ],
         compiler_params=pltpu.CompilerParams(vmem_limit_bytes=PACK_LIMIT << 20),
         name="pack",
     )(live_trades, cashflows, netting_id[None, :], base_yield[None, :], loadings, draws)
-    packs = [shift(packed, "x", by) for by in (2, 1, -1)]
+    packs = [shift(packed, "x", by) for by in (1, -1)]
+    far = shift(half, "x", 2)
+    planes = lax.axis_size("scen")
+    rest = lax.ppermute(far, "scen", [(i, i ^ 1) for i in range(planes)])
     mine = lax.all_to_all(copies, "y", 0, 0, tiled=True)
-    early = pl.pallas_call(
-        unfold_kernel,
-        out_shape=jax.ShapeDtypeStruct((pillars, set_total), jnp.bfloat16),
-        in_specs=[vmem],
+    other = shift(mine, "core", 1)
+    joined = pl.pallas_call(
+        join_kernel,
+        out_shape=jax.ShapeDtypeStruct(packed.shape, packed.dtype),
+        in_specs=[vmem, vmem],
         out_specs=vmem,
         compiler_params=params,
         cost_estimate=pl.CostEstimate(flops=HINT, bytes_accessed=0, transcendentals=0),
-        name="unfold",
-    )(packs[0])
-    mine, early = lax.optimization_barrier((mine, early))
-    other = shift(mine, "core", 1)
-    normals, discount, flow = pl.pallas_call(
+        name="join",
+    )(far, rest)
+    normals, total = pl.pallas_call(
         first_kernel,
         out_shape=(
             jax.ShapeDtypeStruct((part, width), jnp.bfloat16),
-            jax.ShapeDtypeStruct((2 * pillars, part), jnp.bfloat16),
-            jax.ShapeDtypeStruct((2 * pillars, set_total), jnp.bfloat16),
+            jax.ShapeDtypeStruct((set_total, part), jnp.float32),
         ),
-        in_specs=[smem, vmem, vmem, vmem, vmem, vmem],
-        out_specs=(vmem, vmem, vmem),
+        in_specs=[vmem] * 4,
+        out_specs=(vmem, vmem),
         compiler_params=params,
+        cost_estimate=pl.CostEstimate(flops=0, bytes_accessed=0, transcendentals=0),
         name="first",
-    )(lax.axis_index("core").astype(jnp.int32)[None], mine, other, packed, packs[0], early)
+    )(mine, other, packed, joined)
     total = pl.pallas_call(
         price_kernel,
         out_shape=jax.ShapeDtypeStruct((set_total, part), jnp.bfloat16),
-        in_specs=[vmem] * 5,
+        in_specs=[vmem] * 4,
         out_specs=vmem,
         compiler_params=params,
         name="price",
-    )(normals, discount, flow, *packs[1:])
+    )(normals, total, *packs)
     sent = lax.all_to_all(total, TRADE, 0, 0, tiled=True)
     terms = sent.reshape(quarters, groups // quarters, owned, part).astype(jnp.float32)
     net_value = jnp.sum(terms, axis=1).transpose(1, 0, 2).reshape(owned, scen_rows)

time: 84.8 us -> 83.6 us (0.986)
  starting transfers between devices: 29.3 us -> 33.3 us
  waiting for transfers between devices: 26.1 us -> 22.5 us
  Pallas kernels: 7.89 us -> 6.45 us
    all_to_all x1, waiting for transfers between devices: 5.96 us -> 0.01 us  [body(): mine = lax.all_to_all(copies, 'y', 0, 0, tiled=True)]
    ppermute x0 -> x1, starting transfers between devices: none -> 4.27 us  [body(): rest = lax.ppermute(far, 'scen', [(i, i ^ 1) for i in range(planes)])]
    ppermute x0 -> x1, waiting for transfers between devices: none -> 3.54 us  [body(): rest = lax.ppermute(far, 'scen', [(i, i ^ 1) for i in range(planes)])]
    ppermute x4, waiting for transfers between devices: 8.66 us -> 7.41 us  [shift(): lax.ppermute(value, axis, [(i, (i + by) % size) for i in range(size)])]
  transfers between devices with their start and end apart: 6 -> 7, of which waited for: 5 -> 4; matrix products, arithmetic and copies ran while one was open for 0% -> 0% of each run, Pallas kernels for 2% -> 2%
where the time goes in v3:
time: 83.6 us; the launch traced here: 83.2 us
  starting transfers between devices  33.3 us (40%)
  waiting for transfers between devices  22.5 us (27%)
  blocking collectives  18.1 us (22%)
  Pallas kernels  6.45 us (8%)
  between operations  1.46 us (2%)
  other arithmetic  1.31 us (2%)
    all_to_all x1, blocking collectives, everywhere(): return lax.all_to_all(copies, axis, 0, 0, tiled=True)  18.1 us
    all_to_all x1, waiting for transfers between devices, body(): sent = lax.all_to_all(total, TRADE, 0, 0, tiled=True)  11.5 us
    ppermute x4, starting transfers between devices, shift(): lax.ppermute(value, axis, [(i, (i + by) % size) for i in range(size)])  11.2 us
    all_to_all x1, starting transfers between devices, body(): sent = lax.all_to_all(total, TRADE, 0, 0, tiled=True)  10.6 us
    ppermute x4, waiting for transfers between devices, shift(): lax.ppermute(value, axis, [(i, (i + by) % size) for i in range(size)])  7.41 us
    all_to_all x1, starting transfers between devices, body(): mine = lax.all_to_all(copies, 'y', 0, 0, tiled=True)  7.24 us
    ppermute x1, starting transfers between devices, body(): rest = lax.ppermute(far, 'scen', [(i, i ^ 1) for i in range(planes)])  4.27 us
    ppermute x1, waiting for transfers between devices, body(): rest = lax.ppermute(far, 'scen', [(i, i ^ 1) for i in range(planes)])  3.54 us
  transfers between devices with their start and end apart: 7, of which 4 were waited for; matrix products, arithmetic and copies ran while one was open for 0% of the time, Pallas kernels for 2%

profile of v3, /device:TPU:6, one launch (start us, length us, event | category | flops | bytes accessed | tf_op | source)
XLA Modules:
  0.0 83.2 jit_solution(10479388229764065312)
XLA Ops:
  1.3 3.4 %pack.1 = (bf16[80,4224]{1,0:T(8,128)(2,1)}, bf16[80,2176]{1,0:T(8,128)(2,1)}, bf16[8,8,4096]{2,1,0:T(8,128)(2,1)}) custom-call(s32[1]{0:T(128)S(6)} %copy.18.live_ref, bf16[64,2048]{1,0:T(8,128)(2,1)} %cash_hbm.1, s32[1,2048]{1,0:T(1,128)} %bitcast.15, f32[1,64]{1,0:T(1,128)} %bitcast.16, bf16[64,4096]{1,0:T(8,128)(2,1)} %load_hbm.1, ...), custom_call_target="tpu_custom_call" | custom-call | tf_op jit(solution)/shard_map/pack/pallas_call | solution.py:199
  4.7 0.0 copy-start
  4.7 0.0 copy-start.4
  4.7 7.2 %all-to-all-start = ((bf16[8,8,4096]{2,1,0:T(8,128)(2,1)}), bf16[8,8,4096]{2,1,0:T(8,128)(2,1)S(1)}, u32[]{:S(2)}, u32[]{:S(2)}) async-start(bf16[8,8,4096]{2,1,0:T(8,128)(2,1)} %get-tuple-element.7), calls=%async_computation | async-start | bytes 1048576 | tf_op jit(solution)/shard_map/all_to_all | solution.py:224
  12.0 0.0 copy-done.4
  12.0 3.3 %collective-permute-start.1 = (bf16[80,2176]{1,0:T(8,128)(2,1)S(1)}, bf16[80,2176]{1,0:T(8,128)(2,1)S(1)}, u32[]{:S(2)}, u32[]{:S(2)}) collective-permute-start(bf16[80,2176]{1,0:T(8,128)(2,1)S(1)} %copy-done.4), channel_id=1, source_target_pairs={{0,256},{128,384},{256,0},{384,128},{1,257},{129,385},{257,1},{385... | collective-permute-start | bytes 1044488 | tf_op jit(solution)/shard_map/ppermute | solution.py:17
  15.3 0.0 copy-done
  15.3 4.0 %collective-permute-start.3 = (bf16[80,4224]{1,0:T(8,128)(2,1)S(1)}, bf16[80,4224]{1,0:T(8,128)(2,1)S(1)}, u32[]{:S(2)}, u32[]{:S(2)}) collective-permute-start(bf16[80,4224]{1,0:T(8,128)(2,1)S(1)} %copy-done), channel_id=1, source_target_pairs={{0,128},{128,256},{256,384},{384,0},{1,129},{129,257},{257,385},{3... | collective-permute-start | bytes 2027528 | tf_op jit(solution)/shard_map/ppermute | solution.py:17
  19.3 1.9 %collective-permute-start.4 = (bf16[80,4224]{1,0:T(8,128)(2,1)S(1)}, bf16[80,4224]{1,0:T(8,128)(2,1)S(1)}, u32[]{:S(2)}, u32[]{:S(2)}) collective-permute-start(bf16[80,4224]{1,0:T(8,128)(2,1)S(1)} %copy-done), channel_id=1, source_target_pairs={{0,384},{128,0},{256,128},{384,256},{1,385},{129,1},{257,129},{385... | collective-permute-start | bytes 2027528 | tf_op jit(solution)/shard_map/ppermute | solution.py:17
  21.2 5.2 %collective-permute-done.1.near_half = bf16[80,2176]{1,0:T(8,128)(2,1)S(1)} collective-permute-done((bf16[80,2176]{1,0:T(8,128)(2,1)S(1)}, bf16[80,2176]{1,0:T(8,128)(2,1)S(1)}, u32[]{:S(2)}, u32[]{:S(2)}) %collective-permute-start.1) | collective-permute-done | bytes 348192 | tf_op jit(solution)/shard_map/ppermute | solution.py:17
  26.5 4.3 %collective-permute-start.2 = (bf16[80,2176]{1,0:T(8,128)(2,1)S(1)}, bf16[80,2176]{1,0:T(8,128)(2,1)S(1)}, u32[]{:S(2)}, u32[]{:S(2)}) collective-permute-start(bf16[80,2176]{1,0:T(8,128)(2,1)S(1)} %collective-permute-done.1.near_half), channel_id=1, source_target_pairs={{0,1},{1,0},{2,3},{3,2},{4,5},{5,4},{6,7},{7,6},{8,9},{9,8},{10,11... | collective-permute-start | bytes 1044488 | tf_op jit(solution)/shard_map/ppermute | solution.py:223
  30.7 0.0 all-to-all-done.mine_ref
  30.7 1.9 %collective-permute-start = (bf16[8,8,4096]{2,1,0:T(8,128)(2,1)S(1)}, bf16[8,8,4096]{2,1,0:T(8,128)(2,1)S(1)}, u32[]{:S(2)}, u32[]{:S(2)}) collective-permute-start(bf16[8,8,4096]{2,1,0:T(8,128)(2,1)S(1)} %all-to-all-done.mine_ref), channel_id=1, source_target_pairs={{0,8},{8,0},{1,9},{9,1},{2,10},{10,2},{3,11},{11,3},{4,12},{12,4},... | collective-permute-start | bytes 1572872 | tf_op jit(solution)/shard_map/ppermute | solution.py:17
  32.7 3.5 %collective-permute-done.2.next_half = bf16[80,2176]{1,0:T(8,128)(2,1)S(1)} collective-permute-done((bf16[80,2176]{1,0:T(8,128)(2,1)S(1)}, bf16[80,2176]{1,0:T(8,128)(2,1)S(1)}, u32[]{:S(2)}, u32[]{:S(2)}) %collective-permute-start.2) | collective-permute-done | bytes 348192 | tf_op jit(solution)/shard_map/ppermute | solution.py:223
  36.3 0.0 collective-permute-done.other_ref
  36.3 1.2 %first.1 = (bf16[128,4096]{1,0:T(8,128)(2,1)S(1)}, f32[1024,128]{1,0:T(8,128)S(1)}) custom-call(bf16[8,8,4096]{2,1,0:T(8,128)(2,1)S(1)} %all-to-all-done.mine_ref, bf16[8,8,4096]{2,1,0:T(8,128)(2,1)S(1)} %collective-permute-done.other_ref, bf16[80,4224]{1,0:T(8,128)(2,1)S(1)} %copy-done, bf16[80,4224]{1,0:T(8,128)(2,1)S(1)} %join.1.far_ref), custom_call_target="tpu_custom_call" | custom-call | tf_op jit(solution)/shard_map/first/pallas_call | solution.py:235
  37.5 0.0 collective-permute-done.3.refs_0_
  37.5 2.2 %collective-permute-done.4.refs_1_ = bf16[80,4224]{1,0:T(8,128)(2,1)S(1)} collective-permute-done((bf16[80,4224]{1,0:T(8,128)(2,1)S(1)}, bf16[80,4224]{1,0:T(8,128)(2,1)S(1)}, u32[]{:S(2)}, u32[]{:S(2)}) %collective-permute-start.4) | collective-permute-done | bytes 675872 | tf_op jit(solution)/shard_map/ppermute | solution.py:17
  39.7 1.8 %price.1 = bf16[1024,128]{1,0:T(8,128)(2,1)} custom-call(bf16[128,4096]{1,0:T(8,128)(2,1)S(1)} %get-tuple-element.10.normals_ref, f32[1024,128]{1,0:T(8,128)S(1)} %get-tuple-element.11.total_ref, bf16[80,4224]{1,0:T(8,128)(2,1)S(1)} %collective-permute-done.3.refs_0_, bf16[80,4224]{1,0:T(8,128)(2,1)S(1)} %collective-permute-done.4.refs_1_), custom_call_target="tpu_custom_call" | custom-call | tf_op jit(solution)/shard_map/price/pallas_call | solution.py:247
  41.5 0.0 copy-start.3
  41.5 10.6 %all-to-all-start.1 = ((bf16[64,16,128]{2,1,0:T(8,128)(2,1)}), bf16[64,16,128]{2,1,0:T(8,128)(2,1)S(1)}, u32[]{:S(2)}, u32[]{:S(2)}) async-start(bf16[64,16,128]{2,1,0:T(8,128)(2,1)} %bitcast.2), calls=%async_computation.1 | async-start | bytes 524288 | tf_op jit(solution)/shard_map/all_to_all | solution.py:255
  52.1 0.0 copy-done.3
  52.1 0.0 copy-start.1
  52.2 0.0 copy-start.2
  52.2 11.5 %all-to-all-done.1 = bf16[64,16,128]{2,1,0:T(8,128)(2,1)S(1)} async-done(((bf16[64,16,128]{2,1,0:T(8,128)(2,1)}), bf16[64,16,128]{2,1,0:T(8,128)(2,1)S(1)}, u32[]{:S(2)}, u32[]{:S(2)}) %all-to-all-start.1) | async-done | bytes 262176 | tf_op jit(solution)/shard_map/all_to_all | solution.py:255
  63.7 0.0 copy-done.1
  63.7 0.0 copy-done.2
  63.7 0.7 multiply_reduce_fusion
  64.5 18.1 %all_to_all.19 = f32[8,8,128]{2,1,0:T(8,128)S(1)} all-to-all(f32[8,8,128]{2,1,0:T(8,128)S(1)} %broadcast_in_dim_broadcast_in_dim_broadcast_in_dim.3), channel_id=1, replica_groups=mesh['x'=4,'y'=8,'core'=2,'scen'=8] {'scen'}, dimensions={0} | all-to-all | bytes 65536 | tf_op jit(solution)/shard_map/all_to_all | solution.py:23
  82.7 0.5 broadcast_multiply_fusion
  (7 shorter events, 0.1 us)
Async XLA Ops:
  4.7 10.6 %copy-start = (bf16[80,4224]{1,0:T(8,128)(2,1)S(1)}, bf16[80,4224]{1,0:T(8,128)(2,1)}, u32[]{:S(2)}) copy-start(bf16[80,4224]{1,0:T(8,128)(2,1)} %get-tuple-element.8.own_ref) | copy-start | bytes 2027524
  4.7 7.3 %copy-start.4 = (bf16[80,2176]{1,0:T(8,128)(2,1)S(1)}, bf16[80,2176]{1,0:T(8,128)(2,1)}, u32[]{:S(2)}) copy-start(bf16[80,2176]{1,0:T(8,128)(2,1)} %get-tuple-element.9) | copy-start | bytes 1044484
  4.7 26.0 %all-to-all-start = ((bf16[8,8,4096]{2,1,0:T(8,128)(2,1)}), bf16[8,8,4096]{2,1,0:T(8,128)(2,1)S(1)}, u32[]{:S(2)}, u32[]{:S(2)}) async-start(bf16[8,8,4096]{2,1,0:T(8,128)(2,1)} %get-tuple-element.7), calls=%async_computation | async-start | bytes 1048576 | tf_op jit(solution)/shard_map/all_to_all | solution.py:224
  12.0 14.5 %collective-permute-start.1 = (bf16[80,2176]{1,0:T(8,128)(2,1)S(1)}, bf16[80,2176]{1,0:T(8,128)(2,1)S(1)}, u32[]{:S(2)}, u32[]{:S(2)}) collective-permute-start(bf16[80,2176]{1,0:T(8,128)(2,1)S(1)} %copy-done.4), channel_id=1, source_target_pairs={{0,256},{128,384},{256,0},{384,128},{1,257},{129,385},{257,1},{385... | collective-permute-start | bytes 1044488 | tf_op jit(solution)/shard_map/ppermute | solution.py:17
  15.3 22.2 %collective-permute-start.3 = (bf16[80,4224]{1,0:T(8,128)(2,1)S(1)}, bf16[80,4224]{1,0:T(8,128)(2,1)S(1)}, u32[]{:S(2)}, u32[]{:S(2)}) collective-permute-start(bf16[80,4224]{1,0:T(8,128)(2,1)S(1)} %copy-done), channel_id=1, source_target_pairs={{0,128},{128,256},{256,384},{384,0},{1,129},{129,257},{257,385},{3... | collective-permute-start | bytes 2027528 | tf_op jit(solution)/shard_map/ppermute | solution.py:17
  19.3 20.4 %collective-permute-start.4 = (bf16[80,4224]{1,0:T(8,128)(2,1)S(1)}, bf16[80,4224]{1,0:T(8,128)(2,1)S(1)}, u32[]{:S(2)}, u32[]{:S(2)}) collective-permute-start(bf16[80,4224]{1,0:T(8,128)(2,1)S(1)} %copy-done), channel_id=1, source_target_pairs={{0,384},{128,0},{256,128},{384,256},{1,385},{129,1},{257,129},{385... | collective-permute-start | bytes 2027528 | tf_op jit(solution)/shard_map/ppermute | solution.py:17
  26.5 9.8 %collective-permute-start.2 = (bf16[80,2176]{1,0:T(8,128)(2,1)S(1)}, bf16[80,2176]{1,0:T(8,128)(2,1)S(1)}, u32[]{:S(2)}, u32[]{:S(2)}) collective-permute-start(bf16[80,2176]{1,0:T(8,128)(2,1)S(1)} %collective-permute-done.1.near_half), channel_id=1, source_target_pairs={{0,1},{1,0},{2,3},{3,2},{4,5},{5,4},{6,7},{7,6},{8,9},{9,8},{10,11... | collective-permute-start | bytes 1044488 | tf_op jit(solution)/shard_map/ppermute | solution.py:223
  30.7 5.5 %collective-permute-start = (bf16[8,8,4096]{2,1,0:T(8,128)(2,1)S(1)}, bf16[8,8,4096]{2,1,0:T(8,128)(2,1)S(1)}, u32[]{:S(2)}, u32[]{:S(2)}) collective-permute-start(bf16[8,8,4096]{2,1,0:T(8,128)(2,1)S(1)} %all-to-all-done.mine_ref), channel_id=1, source_target_pairs={{0,8},{8,0},{1,9},{9,1},{2,10},{10,2},{3,11},{11,3},{4,12},{12,4},... | collective-permute-start | bytes 1572872 | tf_op jit(solution)/shard_map/ppermute | solution.py:17
  41.5 10.6 %copy-start.3 = (f32[16]{0:T(128)S(1)}, f32[16]{0:T(128)}, u32[]{:S(2)}) copy-start(f32[16]{0:T(128)} %param.17) | copy-start | bytes 196
  41.5 22.2 %all-to-all-start.1 = ((bf16[64,16,128]{2,1,0:T(8,128)(2,1)}), bf16[64,16,128]{2,1,0:T(8,128)(2,1)S(1)}, u32[]{:S(2)}, u32[]{:S(2)}) async-start(bf16[64,16,128]{2,1,0:T(8,128)(2,1)} %bitcast.2), calls=%async_computation.1 | async-start | bytes 524288 | tf_op jit(solution)/shard_map/all_to_all | solution.py:255
  52.1 11.6 %copy-start.1 = (f32[16,512]{1,0:T(8,128)S(1)}, f32[16,512]{1,0:T(8,128)}, u32[]{:S(2)}) copy-start(f32[16,512]{1,0:T(8,128)} %param.16) | copy-start | bytes 98308
  52.2 11.6 %copy-start.2 = (f32[16,512]{1,0:T(8,128)S(1)}, f32[16,512]{1,0:T(8,128)}, u32[]{:S(2)}) copy-start(f32[16,512]{1,0:T(8,128)} %param.15) | copy-start | bytes 98308

commit v4 on v3

--- a/solution.py
+++ b/solution.py
@@ -149,7 +149,20 @@
     )
 
 
-def first_kernel(mine_ref, other_ref, own_ref, far_ref, normals_ref, total_ref):
+def first_kernel(
+    mine_ref, other_ref, own_ref, far_ref, dist_ref, shock_ref, vol_ref,
+    normals_ref, total_ref, crossing_ref
+):
+    owned = dist_ref.shape[0]
+    diagonal = lax.broadcasted_iota(jnp.int32, (owned, owned), 0) == lax.broadcasted_iota(
+        jnp.int32, (owned, owned), 1
+    )
+    spread = jnp.sum(jnp.where(diagonal, vol_ref[...], 0.0), axis=1, keepdims=True)
+    dist_prev = dist_ref[...]
+    dist_now = dist_prev + (0.03 - 0.5 * spread * spread) + spread * shock_ref[...]
+    crossing_ref[...] = jnp.exp(
+        -2.0 * jnp.maximum(dist_prev, 0.0) * jnp.maximum(dist_now, 0.0) / (spread * spread)
+    )
     set_total = total_ref.shape[0]
     width = normals_ref.shape[1]
     pillars = own_ref.shape[0] * width // (width + set_total)
@@ -232,18 +245,19 @@
         cost_estimate=pl.CostEstimate(flops=HINT, bytes_accessed=0, transcendentals=0),
         name="join",
     )(far, rest)
-    normals, total = pl.pallas_call(
+    normals, total, crossing = pl.pallas_call(
         first_kernel,
         out_shape=(
             jax.ShapeDtypeStruct((part, width), jnp.bfloat16),
             jax.ShapeDtypeStruct((set_total, part), jnp.float32),
+            jax.ShapeDtypeStruct(dist_prev.shape, jnp.float32),
         ),
-        in_specs=[vmem] * 4,
-        out_specs=(vmem, vmem),
+        in_specs=[vmem] * 7,
+        out_specs=(vmem, vmem, vmem),
         compiler_params=params,
         cost_estimate=pl.CostEstimate(flops=0, bytes_accessed=0, transcendentals=0),
         name="first",
-    )(mine, other, packed, joined)
+    )(mine, other, packed, joined, dist_prev, shock, vol[None, :])
     total = pl.pallas_call(
         price_kernel,
         out_shape=jax.ShapeDtypeStruct((set_total, part), jnp.bfloat16),
@@ -256,11 +270,6 @@
     terms = sent.reshape(quarters, groups // quarters, owned, part).astype(jnp.float32)
     net_value = jnp.sum(terms, axis=1).transpose(1, 0, 2).reshape(owned, scen_rows)
 
-    spread = vol[:, None]
-    dist_now = dist_prev + (0.03 - 0.5 * spread * spread) + spread * shock
-    crossing = jnp.exp(
-        -2.0 * jnp.maximum(dist_prev, 0.0) * jnp.maximum(dist_now, 0.0) / (spread * spread)
-    )
     losses = jnp.sum(jnp.maximum(net_value, 0.0) * crossing, axis=1)
     tile = jnp.broadcast_to(jnp.pad(losses, (0, LANES - owned)), (8, LANES))
     summed = jnp.sum(everywhere(tile, "scen").reshape(-1, 8, LANES)[:, 0, :owned], axis=0)

time: 83.6 us -> 82.4 us (0.986)
  blocking collectives: 18.1 us -> 40.1 us
  waiting for transfers between devices: 22.5 us -> 8.81 us
  starting transfers between devices: 33.3 us -> 23.8 us
    all_to_all x0 -> x1, blocking collectives: none -> 22 us  [body(): sent = lax.all_to_all(total, TRADE, 0, 0, tiled=True)]
    all_to_all x1 -> x0, waiting for transfers between devices: 11.5 us -> none  [body(): sent = lax.all_to_all(total, TRADE, 0, 0, tiled=True)]
    all_to_all x1 -> x0, starting transfers between devices: 10.6 us -> none  [body(): sent = lax.all_to_all(total, TRADE, 0, 0, tiled=True)]
    ppermute x4, waiting for transfers between devices: 7.41 us -> 5.27 us  [shift(): lax.ppermute(value, axis, [(i, (i + by) % size) for i in range(size)])]
    ppermute x4, starting transfers between devices: 11.2 us -> 12.3 us  [shift(): lax.ppermute(value, axis, [(i, (i + by) % size) for i in range(size)])]
  transfers between devices with their start and end apart: 7 -> 6, of which waited for: 4 -> 3; matrix products, arithmetic and copies ran while one was open for 0% -> 0% of each run, Pallas kernels for 2% -> 2%
where the time goes in v4:
time: 82.4 us; the launch traced here: 82 us
  blocking collectives  40.1 us (49%)
  starting transfers between devices  23.8 us (29%)
  waiting for transfers between devices  8.81 us (11%)
  Pallas kernels  5.84 us (7%)
  between operations  1.44 us (2%)
  other arithmetic  1.3 us (2%)
    all_to_all x1, blocking collectives, body(): sent = lax.all_to_all(total, TRADE, 0, 0, tiled=True)  22 us
    all_to_all x1, blocking collectives, everywhere(): return lax.all_to_all(copies, axis, 0, 0, tiled=True)  18.1 us
    ppermute x4, starting transfers between devices, shift(): lax.ppermute(value, axis, [(i, (i + by) % size) for i in range(size)])  12.3 us
    all_to_all x1, starting transfers between devices, body(): mine = lax.all_to_all(copies, 'y', 0, 0, tiled=True)  7.24 us
    ppermute x4, waiting for transfers between devices, shift(): lax.ppermute(value, axis, [(i, (i + by) % size) for i in range(size)])  5.27 us
    ppermute x1, starting transfers between devices, body(): rest = lax.ppermute(far, 'scen', [(i, i ^ 1) for i in range(planes)])  4.27 us
    ppermute x1, waiting for transfers between devices, body(): rest = lax.ppermute(far, 'scen', [(i, i ^ 1) for i in range(planes)])  3.54 us
    pallas_call x1, Pallas kernels, body(): pl.pallas_call(pack_kernel, out_shape=(jax.ShapeDtypeStruct((pillars + ro...  3.41 us
  transfers between devices with their start and end apart: 6, of which 3 were waited for; matrix products, arithmetic and copies ran while one was open for 0% of the time, Pallas kernels for 2%

profile of v4, /device:TPU:6, one launch (start us, length us, event | category | flops | bytes accessed | tf_op | source)
XLA Modules:
  0.0 82.0 jit_solution(18005207831241230843)
XLA Ops:
  1.3 3.4 %pack.1 = (bf16[80,4224]{1,0:T(8,128)(2,1)}, bf16[80,2176]{1,0:T(8,128)(2,1)}, bf16[8,8,4096]{2,1,0:T(8,128)(2,1)}) custom-call(s32[1]{0:T(128)S(6)} %copy.18.live_ref, bf16[64,2048]{1,0:T(8,128)(2,1)} %cash_hbm.1, s32[1,2048]{1,0:T(1,128)} %bitcast.18, f32[1,64]{1,0:T(1,128)} %bitcast.19, bf16[64,4096]{1,0:T(8,128)(2,1)} %load_hbm.1, ...), custom_call_target="tpu_custom_call" | custom-call | tf_op jit(solution)/shard_map/pack/pallas_call | solution.py:212
  4.7 0.0 copy-start
  4.7 0.0 copy-start.4
  4.7 7.2 %all-to-all-start = ((bf16[8,8,4096]{2,1,0:T(8,128)(2,1)}), bf16[8,8,4096]{2,1,0:T(8,128)(2,1)S(1)}, u32[]{:S(2)}, u32[]{:S(2)}) async-start(bf16[8,8,4096]{2,1,0:T(8,128)(2,1)} %get-tuple-element.8), calls=%async_computation | async-start | bytes 1048576 | tf_op jit(solution)/shard_map/all_to_all | solution.py:237
  12.0 0.0 copy-done.4
  12.0 3.3 %collective-permute-start.1 = (bf16[80,2176]{1,0:T(8,128)(2,1)S(1)}, bf16[80,2176]{1,0:T(8,128)(2,1)S(1)}, u32[]{:S(2)}, u32[]{:S(2)}) collective-permute-start(bf16[80,2176]{1,0:T(8,128)(2,1)S(1)} %copy-done.4), channel_id=1, source_target_pairs={{0,256},{128,384},{256,0},{384,128},{1,257},{129,385},{257,1},{385... | collective-permute-start | bytes 1044488 | tf_op jit(solution)/shard_map/ppermute | solution.py:17
  15.3 0.0 copy-done
  15.3 0.0 copy-start.1
  15.3 0.0 copy-start.2
  15.3 3.6 %collective-permute-start.4 = (bf16[80,4224]{1,0:T(8,128)(2,1)S(1)}, bf16[80,4224]{1,0:T(8,128)(2,1)S(1)}, u32[]{:S(2)}, u32[]{:S(2)}) collective-permute-start(bf16[80,4224]{1,0:T(8,128)(2,1)S(1)} %copy-done), channel_id=1, source_target_pairs={{0,384},{128,0},{256,128},{384,256},{1,385},{129,1},{257,129},{385... | collective-permute-start | bytes 2027528 | tf_op jit(solution)/shard_map/ppermute | solution.py:17
  18.9 3.4 %collective-permute-start.3 = (bf16[80,4224]{1,0:T(8,128)(2,1)S(1)}, bf16[80,4224]{1,0:T(8,128)(2,1)S(1)}, u32[]{:S(2)}, u32[]{:S(2)}) collective-permute-start(bf16[80,4224]{1,0:T(8,128)(2,1)S(1)} %copy-done), channel_id=1, source_target_pairs={{0,128},{128,256},{256,384},{384,0},{1,129},{129,257},{257,385},{3... | collective-permute-start | bytes 2027528 | tf_op jit(solution)/shard_map/ppermute | solution.py:17
  22.4 4.1 %collective-permute-done.1.near_half = bf16[80,2176]{1,0:T(8,128)(2,1)S(1)} collective-permute-done((bf16[80,2176]{1,0:T(8,128)(2,1)S(1)}, bf16[80,2176]{1,0:T(8,128)(2,1)S(1)}, u32[]{:S(2)}, u32[]{:S(2)}) %collective-permute-start.1) | collective-permute-done | bytes 348192 | tf_op jit(solution)/shard_map/ppermute | solution.py:17
  26.5 4.3 %collective-permute-start.2 = (bf16[80,2176]{1,0:T(8,128)(2,1)S(1)}, bf16[80,2176]{1,0:T(8,128)(2,1)S(1)}, u32[]{:S(2)}, u32[]{:S(2)}) collective-permute-start(bf16[80,2176]{1,0:T(8,128)(2,1)S(1)} %collective-permute-done.1.near_half), channel_id=1, source_target_pairs={{0,1},{1,0},{2,3},{3,2},{4,5},{5,4},{6,7},{7,6},{8,9},{9,8},{10,11... | collective-permute-start | bytes 1044488 | tf_op jit(solution)/shard_map/ppermute | solution.py:236
  30.8 0.0 all-to-all-done.mine_ref
  30.8 1.9 %collective-permute-start = (bf16[8,8,4096]{2,1,0:T(8,128)(2,1)S(1)}, bf16[8,8,4096]{2,1,0:T(8,128)(2,1)S(1)}, u32[]{:S(2)}, u32[]{:S(2)}) collective-permute-start(bf16[8,8,4096]{2,1,0:T(8,128)(2,1)S(1)} %all-to-all-done.mine_ref), channel_id=1, source_target_pairs={{0,8},{8,0},{1,9},{9,1},{2,10},{10,2},{3,11},{11,3},{4,12},{12,4},... | collective-permute-start | bytes 1572872 | tf_op jit(solution)/shard_map/ppermute | solution.py:17
  32.7 3.5 %collective-permute-done.2.next_half = bf16[80,2176]{1,0:T(8,128)(2,1)S(1)} collective-permute-done((bf16[80,2176]{1,0:T(8,128)(2,1)S(1)}, bf16[80,2176]{1,0:T(8,128)(2,1)S(1)}, u32[]{:S(2)}, u32[]{:S(2)}) %collective-permute-start.2) | collective-permute-done | bytes 348192 | tf_op jit(solution)/shard_map/ppermute | solution.py:236
  36.3 0.0 copy-start.3
  36.3 0.0 collective-permute-done.other_ref
  36.3 0.0 copy-done.1
  36.3 0.0 copy-done.2
  36.3 0.6 copy-done.3
  37.0 1.3 %first.1 = (bf16[128,4096]{1,0:T(8,128)(2,1)S(1)}, f32[1024,128]{1,0:T(8,128)S(1)}, f32[16,512]{1,0:T(8,128)S(1)}) custom-call(bf16[8,8,4096]{2,1,0:T(8,128)(2,1)S(1)} %all-to-all-done.mine_ref, bf16[8,8,4096]{2,1,0:T(8,128)(2,1)S(1)} %collective-permute-done.other_ref, bf16[80,4224]{1,0:T(8,128)(2,1)S(1)} %copy-done, bf16[80,4224]{1,0:T(8,128)(2,1)S(1)} %join.1.far_ref, ...), custom_call_target="tpu_custom_call" | custom-call | tf_op jit(solution)/shard_map/first/pallas_call | solution.py:248
  38.3 1.2 %collective-permute-done.4.refs_1_ = bf16[80,4224]{1,0:T(8,128)(2,1)S(1)} collective-permute-done((bf16[80,4224]{1,0:T(8,128)(2,1)S(1)}, bf16[80,4224]{1,0:T(8,128)(2,1)S(1)}, u32[]{:S(2)}, u32[]{:S(2)}) %collective-permute-start.4) | collective-permute-done | bytes 675872 | tf_op jit(solution)/shard_map/ppermute | solution.py:17
  39.5 0.0 collective-permute-done.3.refs_0_
  39.5 1.1 %price.1 = bf16[1024,128]{1,0:T(8,128)(2,1)S(1)} custom-call(bf16[128,4096]{1,0:T(8,128)(2,1)S(1)} %get-tuple-element.11.normals_ref, f32[1024,128]{1,0:T(8,128)S(1)} %get-tuple-element.12.total_ref, bf16[80,4224]{1,0:T(8,128)(2,1)S(1)} %collective-permute-done.3.refs_0_, bf16[80,4224]{1,0:T(8,128)(2,1)S(1)} %collective-permute-done.4.refs_1_), custom_call_target="tpu_custom_call" | custom-call | tf_op jit(solution)/shard_map/price/pallas_call | solution.py:261
  40.5 22.0 %all_to_all.19 = bf16[64,16,128]{2,1,0:T(8,128)(2,1)S(1)} all-to-all(bf16[64,16,128]{2,1,0:T(8,128)(2,1)S(1)} %bitcast.15), channel_id=1, replica_groups=mesh['x'=4,'y'=8,'core'=2,'scen'=8] {'x','y','core'}, dimensions={0} | all-to-all | bytes 524288 | tf_op jit(solution)/shard_map/all_to_all | solution.py:269
  62.5 0.7 multiply_reduce_fusion
  63.3 18.1 %all_to_all.20 = f32[8,8,128]{2,1,0:T(8,128)S(1)} all-to-all(f32[8,8,128]{2,1,0:T(8,128)S(1)} %broadcast_in_dim_broadcast_in_dim_broadcast_in_dim.3), channel_id=1, replica_groups=mesh['x'=4,'y'=8,'core'=2,'scen'=8] {'scen'}, dimensions={0} | all-to-all | bytes 65536 | tf_op jit(solution)/shard_map/all_to_all | solution.py:23
  81.4 0.5 broadcast_multiply_fusion
  (6 shorter events, 0.1 us)
Async XLA Ops:
  4.7 10.6 %copy-start = (bf16[80,4224]{1,0:T(8,128)(2,1)S(1)}, bf16[80,4224]{1,0:T(8,128)(2,1)}, u32[]{:S(2)}) copy-start(bf16[80,4224]{1,0:T(8,128)(2,1)} %get-tuple-element.9.own_ref) | copy-start | bytes 2027524
  4.7 7.3 %copy-start.4 = (bf16[80,2176]{1,0:T(8,128)(2,1)S(1)}, bf16[80,2176]{1,0:T(8,128)(2,1)}, u32[]{:S(2)}) copy-start(bf16[80,2176]{1,0:T(8,128)(2,1)} %get-tuple-element.10) | copy-start | bytes 1044484
  4.7 26.0 %all-to-all-start = ((bf16[8,8,4096]{2,1,0:T(8,128)(2,1)}), bf16[8,8,4096]{2,1,0:T(8,128)(2,1)S(1)}, u32[]{:S(2)}, u32[]{:S(2)}) async-start(bf16[8,8,4096]{2,1,0:T(8,128)(2,1)} %get-tuple-element.8), calls=%async_computation | async-start | bytes 1048576 | tf_op jit(solution)/shard_map/all_to_all | solution.py:237
  12.0 14.5 %collective-permute-start.1 = (bf16[80,2176]{1,0:T(8,128)(2,1)S(1)}, bf16[80,2176]{1,0:T(8,128)(2,1)S(1)}, u32[]{:S(2)}, u32[]{:S(2)}) collective-permute-start(bf16[80,2176]{1,0:T(8,128)(2,1)S(1)} %copy-done.4), channel_id=1, source_target_pairs={{0,256},{128,384},{256,0},{384,128},{1,257},{129,385},{257,1},{385... | collective-permute-start | bytes 1044488 | tf_op jit(solution)/shard_map/ppermute | solution.py:17
  15.3 21.0 %copy-start.1 = (f32[16,512]{1,0:T(8,128)S(1)}, f32[16,512]{1,0:T(8,128)}, u32[]{:S(2)}) copy-start(f32[16,512]{1,0:T(8,128)} %dist_ref.1) | copy-start | bytes 98308
  15.3 21.0 %copy-start.2 = (f32[16,512]{1,0:T(8,128)S(1)}, f32[16,512]{1,0:T(8,128)}, u32[]{:S(2)}) copy-start(f32[16,512]{1,0:T(8,128)} %shock_ref.1) | copy-start | bytes 98308
  15.3 24.1 %collective-permute-start.4 = (bf16[80,4224]{1,0:T(8,128)(2,1)S(1)}, bf16[80,4224]{1,0:T(8,128)(2,1)S(1)}, u32[]{:S(2)}, u32[]{:S(2)}) collective-permute-start(bf16[80,4224]{1,0:T(8,128)(2,1)S(1)} %copy-done), channel_id=1, source_target_pairs={{0,384},{128,0},{256,128},{384,256},{1,385},{129,1},{257,129},{385... | collective-permute-start | bytes 2027528 | tf_op jit(solution)/shard_map/ppermute | solution.py:17
  18.9 20.5 %collective-permute-start.3 = (bf16[80,4224]{1,0:T(8,128)(2,1)S(1)}, bf16[80,4224]{1,0:T(8,128)(2,1)S(1)}, u32[]{:S(2)}, u32[]{:S(2)}) collective-permute-start(bf16[80,4224]{1,0:T(8,128)(2,1)S(1)} %copy-done), channel_id=1, source_target_pairs={{0,128},{128,256},{256,384},{384,0},{1,129},{129,257},{257,385},{3... | collective-permute-start | bytes 2027528 | tf_op jit(solution)/shard_map/ppermute | solution.py:17
  26.5 9.8 %collective-permute-start.2 = (bf16[80,2176]{1,0:T(8,128)(2,1)S(1)}, bf16[80,2176]{1,0:T(8,128)(2,1)S(1)}, u32[]{:S(2)}, u32[]{:S(2)}) collective-permute-start(bf16[80,2176]{1,0:T(8,128)(2,1)S(1)} %collective-permute-done.1.near_half), channel_id=1, source_target_pairs={{0,1},{1,0},{2,3},{3,2},{4,5},{5,4},{6,7},{7,6},{8,9},{9,8},{10,11... | collective-permute-start | bytes 1044488 | tf_op jit(solution)/shard_map/ppermute | solution.py:236
  30.8 5.5 %collective-permute-start = (bf16[8,8,4096]{2,1,0:T(8,128)(2,1)S(1)}, bf16[8,8,4096]{2,1,0:T(8,128)(2,1)S(1)}, u32[]{:S(2)}, u32[]{:S(2)}) collective-permute-start(bf16[8,8,4096]{2,1,0:T(8,128)(2,1)S(1)} %all-to-all-done.mine_ref), channel_id=1, source_target_pairs={{0,8},{8,0},{1,9},{9,1},{2,10},{10,2},{3,11},{11,3},{4,12},{12,4},... | collective-permute-start | bytes 1572872 | tf_op jit(solution)/shard_map/ppermute | solution.py:17
  36.3 0.7 copy-start.3

commit v5 on v3

--- a/solution.py
+++ b/solution.py
@@ -6,6 +6,7 @@
 from jax.sharding import Mesh, PartitionSpec as P
 
 LANES = 128
+HOLD = 8 * 10**9
 HINT = 25 * 10**8
 LIMIT = 16
 PACK_LIMIT = 62
@@ -65,6 +66,11 @@
     ]
     for move in moves:
         move.start()
+    def members(first):
+        numbers = first + lax.broadcasted_iota(jnp.int32, (256, trades), 0)
+        return jnp.where(numbers == owner, 1.0, 0.0).astype(jnp.bfloat16)
+
+    member = members(0)
     cash_in.wait()
     load_in.wait()
     load_out = pltpu.make_async_copy(load_ref, out_hbm.at[pl.ds(0, pillars)], sems.at[3])
@@ -76,8 +82,8 @@
     )
     load_half.start()
     for first in range(0, set_total, 256):
-        numbers = first + lax.broadcasted_iota(jnp.int32, (256, trades), 0)
-        member = jnp.where(numbers == owner, 1.0, 0.0).astype(jnp.bfloat16)
+        if first > 0:
+            member = members(first)
         flows = lax.dot_general(
             cash_ref[...], member, (((1,), (1,)), ((), ())), preferred_element_type=jnp.float32
         ).astype(jnp.bfloat16)
@@ -123,7 +129,25 @@
     )
 
 
-def join_kernel(near_half, next_half, out_ref):
+def hold_kernel(half_ref, out_ref):
+    del half_ref
+    out_ref[...] = jnp.zeros_like(out_ref)
+
+
+def join_kernel(
+    near_half, next_half, held_ref, dist_ref, shock_ref, vol_ref, out_ref, crossing_ref
+):
+    del held_ref
+    owned = dist_ref.shape[0]
+    diagonal = lax.broadcasted_iota(jnp.int32, (owned, owned), 0) == lax.broadcasted_iota(
+        jnp.int32, (owned, owned), 1
+    )
+    spread = jnp.sum(jnp.where(diagonal, vol_ref[...], 0.0), axis=1, keepdims=True)
+    dist_prev = dist_ref[...]
+    dist_now = dist_prev + (0.03 - 0.5 * spread * spread) + spread * shock_ref[...]
+    crossing_ref[...] = jnp.exp(
+        -2.0 * jnp.maximum(dist_prev, 0.0) * jnp.maximum(dist_now, 0.0) / (spread * spread)
+    )
     middle = out_ref.shape[1] - near_half.shape[1]
     even = lax.rem(lax.axis_index("scen"), 2) == 0
 
@@ -149,7 +173,9 @@
     )
 
 
-def first_kernel(mine_ref, other_ref, own_ref, far_ref, normals_ref, total_ref):
+def first_kernel(
+    mine_ref, other_ref, own_ref, far_ref, normals_ref, total_ref
+):
     set_total = total_ref.shape[0]
     width = normals_ref.shape[1]
     pillars = own_ref.shape[0] * width // (width + set_total)
@@ -219,19 +245,32 @@
     )(live_trades, cashflows, netting_id[None, :], base_yield[None, :], loadings, draws)
     packs = [shift(packed, "x", by) for by in (1, -1)]
     far = shift(half, "x", 2)
+    held = pl.pallas_call(
+        hold_kernel,
+        out_shape=jax.ShapeDtypeStruct((8, LANES), jnp.float32),
+        in_specs=[pl.BlockSpec(memory_space=pl.ANY)],
+        out_specs=vmem,
+        compiler_params=params,
+        cost_estimate=pl.CostEstimate(flops=HOLD, bytes_accessed=0, transcendentals=0),
+        name="hold",
+    )(far)
+    far, held = lax.optimization_barrier((far, held))
     planes = lax.axis_size("scen")
     rest = lax.ppermute(far, "scen", [(i, i ^ 1) for i in range(planes)])
     mine = lax.all_to_all(copies, "y", 0, 0, tiled=True)
     other = shift(mine, "core", 1)
-    joined = pl.pallas_call(
+    joined, crossing = pl.pallas_call(
         join_kernel,
-        out_shape=jax.ShapeDtypeStruct(packed.shape, packed.dtype),
-        in_specs=[vmem, vmem],
-        out_specs=vmem,
+        out_shape=(
+            jax.ShapeDtypeStruct(packed.shape, packed.dtype),
+            jax.ShapeDtypeStruct(dist_prev.shape, jnp.float32),
+        ),
+        in_specs=[vmem] * 6,
+        out_specs=(vmem, vmem),
         compiler_params=params,
         cost_estimate=pl.CostEstimate(flops=HINT, bytes_accessed=0, transcendentals=0),
         name="join",
-    )(far, rest)
+    )(far, rest, held, dist_prev, shock, vol[None, :])
     normals, total = pl.pallas_call(
         first_kernel,
         out_shape=(
@@ -256,14 +295,9 @@
     terms = sent.reshape(quarters, groups // quarters, owned, part).astype(jnp.float32)
     net_value = jnp.sum(terms, axis=1).transpose(1, 0, 2).reshape(owned, scen_rows)
 
-    spread = vol[:, None]
-    dist_now = dist_prev + (0.03 - 0.5 * spread * spread) + spread * shock
-    crossing = jnp.exp(
-        -2.0 * jnp.maximum(dist_prev, 0.0) * jnp.maximum(dist_now, 0.0) / (spread * spread)
-    )
     losses = jnp.sum(jnp.maximum(net_value, 0.0) * crossing, axis=1)
-    tile = jnp.broadcast_to(jnp.pad(losses, (0, LANES - owned)), (8, LANES))
-    summed = jnp.sum(everywhere(tile, "scen").reshape(-1, 8, LANES)[:, 0, :owned], axis=0)
+    tile = jnp.pad(losses, (0, LANES - owned))[None]
+    summed = jnp.sum(everywhere(tile, "scen").reshape(-1, LANES)[:, :owned], axis=0)
     expected_loss = summed / (scen_rows * lax.axis_size("scen"))
     return (net_value, expected_loss)
 

time: 83.6 us -> 79.5 us (0.951)
  blocking collectives: 18.1 us -> 39.1 us
  waiting for transfers between devices: 22.5 us -> 7.49 us
  starting transfers between devices: 33.3 us -> 23.8 us
    all_to_all x0 -> x1, blocking collectives: none -> 21.3 us  [body(): sent = lax.all_to_all(total, TRADE, 0, 0, tiled=True)]
    all_to_all x1 -> x0, waiting for transfers between devices: 11.5 us -> none  [body(): sent = lax.all_to_all(total, TRADE, 0, 0, tiled=True)]
    all_to_all x1 -> x0, starting transfers between devices: 10.6 us -> none  [body(): sent = lax.all_to_all(total, TRADE, 0, 0, tiled=True)]
    all_to_all x1, waiting for transfers between devices: 0.01 us -> 5.79 us  [body(): mine = lax.all_to_all(copies, 'y', 0, 0, tiled=True)]
    ppermute x4, waiting for transfers between devices: 7.41 us -> 1.7 us  [shift(): lax.ppermute(value, axis, [(i, (i + by) % size) for i in range(size)])]
    ppermute x1, waiting for transfers between devices: 3.54 us -> 0.01 us  [body(): rest = lax.ppermute(far, 'scen', [(i, i ^ 1) for i in range(planes)])]
    ppermute x4, starting transfers between devices: 11.2 us -> 12.4 us  [shift(): lax.ppermute(value, axis, [(i, (i + by) % size) for i in range(size)])]
  transfers between devices with their start and end apart: 7 -> 6, of which waited for: 4 -> 2; matrix products, arithmetic and copies ran while one was open for 0% -> 0% of each run, Pallas kernels for 2% -> 2%
where the time goes in v5:
time: 79.5 us; the launch traced here: 79 us
  blocking collectives  39.1 us (49%)
  starting transfers between devices  23.8 us (30%)
  waiting for transfers between devices  7.49 us (9%)
  Pallas kernels  5.82 us (7%)
  between operations  1.46 us (2%)
  other arithmetic  1.3 us (2%)
    all_to_all x1, blocking collectives, body(): sent = lax.all_to_all(total, TRADE, 0, 0, tiled=True)  21.3 us
    all_to_all x1, blocking collectives, everywhere(): return lax.all_to_all(copies, axis, 0, 0, tiled=True)  17.8 us
    ppermute x4, starting transfers between devices, shift(): lax.ppermute(value, axis, [(i, (i + by) % size) for i in range(size)])  12.4 us
    all_to_all x1, starting transfers between devices, body(): mine = lax.all_to_all(copies, 'y', 0, 0, tiled=True)  7.12 us
    all_to_all x1, waiting for transfers between devices, body(): mine = lax.all_to_all(copies, 'y', 0, 0, tiled=True)  5.79 us
    ppermute x1, starting transfers between devices, body(): rest = lax.ppermute(far, 'scen', [(i, i ^ 1) for i in range(planes)])  4.28 us
    pallas_call x1, Pallas kernels, body(): pl.pallas_call(pack_kernel, out_shape=(jax.ShapeDtypeStruct((pillars + ro...  3.43 us
    ppermute x4, waiting for transfers between devices, shift(): lax.ppermute(value, axis, [(i, (i + by) % size) for i in range(size)])  1.7 us
  transfers between devices with their start and end apart: 6, of which 2 were waited for; matrix products, arithmetic and copies ran while one was open for 0% of the time, Pallas kernels for 2%

profile of v5, /device:TPU:6, one launch (start us, length us, event | category | flops | bytes accessed | tf_op | source)
XLA Modules:
  0.0 79.0 jit_solution(16035380234608505545)
XLA Ops:
  1.3 3.4 %pack.1 = (bf16[80,4224]{1,0:T(8,128)(2,1)}, bf16[80,2176]{1,0:T(8,128)(2,1)}, bf16[8,8,4096]{2,1,0:T(8,128)(2,1)}) custom-call(s32[1]{0:T(128)S(6)} %copy.17.live_ref, bf16[64,2048]{1,0:T(8,128)(2,1)} %cash_hbm.1, s32[1,2048]{1,0:T(1,128)} %bitcast.18, f32[1,64]{1,0:T(1,128)} %bitcast.19, bf16[64,4096]{1,0:T(8,128)(2,1)} %load_hbm.1, ...), custom_call_target="tpu_custom_call" | custom-call | tf_op jit(solution)/shard_map/pack/pallas_call | solution.py:225
  4.7 0.0 copy-start
  4.7 3.4 %collective-permute-start.1 = (bf16[80,2176]{1,0:T(8,128)(2,1)}, bf16[80,2176]{1,0:T(8,128)(2,1)S(1)}, u32[]{:S(2)}, u32[]{:S(2)}) collective-permute-start(bf16[80,2176]{1,0:T(8,128)(2,1)} %get-tuple-element.13), channel_id=1, source_target_pairs={{0,256},{128,384},{256,0},{384,128},{1,257},{129,385},{257,1},{385... | collective-permute-start | bytes 1044488 | tf_op jit(solution)/shard_map/ppermute | solution.py:18
  8.2 7.1 %all-to-all-start = ((bf16[8,8,4096]{2,1,0:T(8,128)(2,1)}), bf16[8,8,4096]{2,1,0:T(8,128)(2,1)S(1)}, u32[]{:S(2)}, u32[]{:S(2)}) async-start(bf16[8,8,4096]{2,1,0:T(8,128)(2,1)} %get-tuple-element.11), calls=%async_computation | async-start | bytes 1048576 | tf_op jit(solution)/shard_map/all_to_all | solution.py:260
  15.3 0.0 copy-done
  15.3 0.0 copy-start.1
  15.3 0.0 copy-start.2
  15.3 3.6 %collective-permute-start.4 = (bf16[80,4224]{1,0:T(8,128)(2,1)S(1)}, bf16[80,4224]{1,0:T(8,128)(2,1)S(1)}, u32[]{:S(2)}, u32[]{:S(2)}) collective-permute-start(bf16[80,4224]{1,0:T(8,128)(2,1)S(1)} %copy-done), channel_id=1, source_target_pairs={{0,384},{128,0},{256,128},{384,256},{1,385},{129,1},{257,129},{385... | collective-permute-start | bytes 2027528 | tf_op jit(solution)/shard_map/ppermute | solution.py:18
  18.9 3.4 %collective-permute-start.3 = (bf16[80,4224]{1,0:T(8,128)(2,1)S(1)}, bf16[80,4224]{1,0:T(8,128)(2,1)S(1)}, u32[]{:S(2)}, u32[]{:S(2)}) collective-permute-start(bf16[80,4224]{1,0:T(8,128)(2,1)S(1)} %copy-done), channel_id=1, source_target_pairs={{0,128},{128,256},{256,384},{384,0},{1,129},{129,257},{257,385},{3... | collective-permute-start | bytes 2027528 | tf_op jit(solution)/shard_map/ppermute | solution.py:18
  22.4 0.0 collective-permute-done.1.half_ref.near_half
  22.4 0.0 copy-start.3
  22.4 4.3 %collective-permute-start.2 = (bf16[80,2176]{1,0:T(8,128)(2,1)S(1)}, bf16[80,2176]{1,0:T(8,128)(2,1)S(1)}, u32[]{:S(2)}, u32[]{:S(2)}) collective-permute-start(bf16[80,2176]{1,0:T(8,128)(2,1)S(1)} %collective-permute-done.1.half_ref.near_half), channel_id=1, source_target_pairs={{0,1},{1,0},{2,3},{3,2},{4,5},{5,4},{6,7},{7,6},{8,9},{9,8},{10,11... | collective-permute-start | bytes 1044488 | tf_op jit(solution)/shard_map/ppermute | solution.py:259
  26.7 5.8 %all-to-all-done.mine_ref = bf16[8,8,4096]{2,1,0:T(8,128)(2,1)S(1)} async-done(((bf16[8,8,4096]{2,1,0:T(8,128)(2,1)}), bf16[8,8,4096]{2,1,0:T(8,128)(2,1)S(1)}, u32[]{:S(2)}, u32[]{:S(2)}) %all-to-all-start) | async-done | bytes 524320 | tf_op jit(solution)/shard_map/all_to_all | solution.py:260
  32.5 1.9 %collective-permute-start = (bf16[8,8,4096]{2,1,0:T(8,128)(2,1)S(1)}, bf16[8,8,4096]{2,1,0:T(8,128)(2,1)S(1)}, u32[]{:S(2)}, u32[]{:S(2)}) collective-permute-start(bf16[8,8,4096]{2,1,0:T(8,128)(2,1)S(1)} %all-to-all-done.mine_ref), channel_id=1, source_target_pairs={{0,8},{8,0},{1,9},{9,1},{2,10},{10,2},{3,11},{11,3},{4,12},{12,4},... | collective-permute-start | bytes 1572872 | tf_op jit(solution)/shard_map/ppermute | solution.py:18
  34.4 0.0 collective-permute-done.2.next_half
  34.4 0.0 copy-done.1
  34.4 0.0 copy-done.2
  34.4 0.0 copy-done.3
  34.5 0.1 join.1
  34.6 1.7 %collective-permute-done.other_ref = bf16[8,8,4096]{2,1,0:T(8,128)(2,1)S(1)} collective-permute-done((bf16[8,8,4096]{2,1,0:T(8,128)(2,1)S(1)}, bf16[8,8,4096]{2,1,0:T(8,128)(2,1)S(1)}, u32[]{:S(2)}, u32[]{:S(2)}) %collective-permute-start) | collective-permute-done | bytes 524320 | tf_op jit(solution)/shard_map/ppermute | solution.py:18
  36.3 1.2 %first.1 = (bf16[128,4096]{1,0:T(8,128)(2,1)S(1)}, f32[1024,128]{1,0:T(8,128)S(1)}) custom-call(bf16[8,8,4096]{2,1,0:T(8,128)(2,1)S(1)} %all-to-all-done.mine_ref, bf16[8,8,4096]{2,1,0:T(8,128)(2,1)S(1)} %collective-permute-done.other_ref, bf16[80,4224]{1,0:T(8,128)(2,1)S(1)} %copy-done, bf16[80,4224]{1,0:T(8,128)(2,1)S(1)} %get-tuple-element.16.far_ref), custom_call_target="tpu_custom_call" | custom-call | tf_op jit(solution)/shard_map/first/pallas_call | solution.py:274
  37.5 0.0 collective-permute-done.4.refs_1_
  37.5 0.0 collective-permute-done.3.refs_0_
  37.5 1.1 %price.1 = bf16[1024,128]{1,0:T(8,128)(2,1)S(1)} custom-call(bf16[128,4096]{1,0:T(8,128)(2,1)S(1)} %get-tuple-element.17.normals_ref, f32[1024,128]{1,0:T(8,128)S(1)} %get-tuple-element.18.total_ref, bf16[80,4224]{1,0:T(8,128)(2,1)S(1)} %collective-permute-done.3.refs_0_, bf16[80,4224]{1,0:T(8,128)(2,1)S(1)} %collective-permute-done.4.refs_1_), custom_call_target="tpu_custom_call" | custom-call | tf_op jit(solution)/shard_map/price/pallas_call | solution.py:286
  38.6 21.3 %all_to_all.19 = bf16[64,16,128]{2,1,0:T(8,128)(2,1)S(1)} all-to-all(bf16[64,16,128]{2,1,0:T(8,128)(2,1)S(1)} %bitcast.15), channel_id=1, replica_groups=mesh['x'=4,'y'=8,'core'=2,'scen'=8] {'x','y','core'}, dimensions={0} | all-to-all | bytes 524288 | tf_op jit(solution)/shard_map/all_to_all | solution.py:294
  59.9 0.7 multiply_reduce_fusion
  60.7 17.8 %all_to_all.20 = f32[8,1,128]{2,1,0:T(1,128)S(1)} all-to-all(f32[8,1,128]{2,1,0:T(1,128)S(1)} %broadcast_in_dim.17), channel_id=1, replica_groups=mesh['x'=4,'y'=8,'core'=2,'scen'=8] {'scen'}, dimensions={0} | all-to-all | bytes 8192 | tf_op jit(solution)/shard_map/all_to_all | solution.py:24
  78.5 0.5 broadcast_multiply_fusion
  (5 shorter events, 0.1 us)
Async XLA Ops:
  4.7 10.6 %copy-start = (bf16[80,4224]{1,0:T(8,128)(2,1)S(1)}, bf16[80,4224]{1,0:T(8,128)(2,1)}, u32[]{:S(2)}) copy-start(bf16[80,4224]{1,0:T(8,128)(2,1)} %get-tuple-element.12.own_ref) | copy-start | bytes 2027524
  4.7 17.7 %collective-permute-start.1 = (bf16[80,2176]{1,0:T(8,128)(2,1)}, bf16[80,2176]{1,0:T(8,128)(2,1)S(1)}, u32[]{:S(2)}, u32[]{:S(2)}) collective-permute-start(bf16[80,2176]{1,0:T(8,128)(2,1)} %get-tuple-element.13), channel_id=1, source_target_pairs={{0,256},{128,384},{256,0},{384,128},{1,257},{129,385},{257,1},{385... | collective-permute-start | bytes 1044488 | tf_op jit(solution)/shard_map/ppermute | solution.py:18
  8.2 24.3 %all-to-all-start = ((bf16[8,8,4096]{2,1,0:T(8,128)(2,1)}), bf16[8,8,4096]{2,1,0:T(8,128)(2,1)S(1)}, u32[]{:S(2)}, u32[]{:S(2)}) async-start(bf16[8,8,4096]{2,1,0:T(8,128)(2,1)} %get-tuple-element.11), calls=%async_computation | async-start | bytes 1048576 | tf_op jit(solution)/shard_map/all_to_all | solution.py:260
  15.3 19.1 %copy-start.1 = (f32[16,512]{1,0:T(8,128)S(1)}, f32[16,512]{1,0:T(8,128)}, u32[]{:S(2)}) copy-start(f32[16,512]{1,0:T(8,128)} %dist_ref.1) | copy-start | bytes 98308
  15.3 19.1 %copy-start.2 = (f32[16,512]{1,0:T(8,128)S(1)}, f32[16,512]{1,0:T(8,128)}, u32[]{:S(2)}) copy-start(f32[16,512]{1,0:T(8,128)} %shock_ref.1) | copy-start | bytes 98308
  15.3 22.2 %collective-permute-start.4 = (bf16[80,4224]{1,0:T(8,128)(2,1)S(1)}, bf16[80,4224]{1,0:T(8,128)(2,1)S(1)}, u32[]{:S(2)}, u32[]{:S(2)}) collective-permute-start(bf16[80,4224]{1,0:T(8,128)(2,1)S(1)} %copy-done), channel_id=1, source_target_pairs={{0,384},{128,0},{256,128},{384,256},{1,385},{129,1},{257,129},{385... | collective-permute-start | bytes 2027528 | tf_op jit(solution)/shard_map/ppermute | solution.py:18
  18.9 18.6 %collective-permute-start.3 = (bf16[80,4224]{1,0:T(8,128)(2,1)S(1)}, bf16[80,4224]{1,0:T(8,128)(2,1)S(1)}, u32[]{:S(2)}, u32[]{:S(2)}) collective-permute-start(bf16[80,4224]{1,0:T(8,128)(2,1)S(1)} %copy-done), channel_id=1, source_target_pairs={{0,128},{128,256},{256,384},{384,0},{1,129},{129,257},{257,385},{3... | collective-permute-start | bytes 2027528 | tf_op jit(solution)/shard_map/ppermute | solution.py:18
  22.4 12.0 %copy-start.3 = (f32[16]{0:T(128)S(1)}, f32[16]{0:T(128)}, u32[]{:S(2)}) copy-start(f32[16]{0:T(128)} %param.17) | copy-start | bytes 196
  22.4 12.0 %collective-permute-start.2 = (bf16[80,2176]{1,0:T(8,128)(2,1)S(1)}, bf16[80,2176]{1,0:T(8,128)(2,1)S(1)}, u32[]{:S(2)}, u32[]{:S(2)}) collective-permute-start(bf16[80,2176]{1,0:T(8,128)(2,1)S(1)} %collective-permute-done.1.half_ref.near_half), channel_id=1, source_target_pairs={{0,1},{1,0},{2,3},{3,2},{4,5},{5,4},{6,7},{7,6},{8,9},{9,8},{10,11... | collective-permute-start | bytes 1044488 | tf_op jit(solution)/shard_map/ppermute | solution.py:259
  32.5 3.8 %collective-permute-start = (bf16[8,8,4096]{2,1,0:T(8,128)(2,1)S(1)}, bf16[8,8,4096]{2,1,0:T(8,128)(2,1)S(1)}, u32[]{:S(2)}, u32[]{:S(2)}) collective-permute-start(bf16[8,8,4096]{2,1,0:T(8,128)(2,1)S(1)} %all-to-all-done.mine_ref), channel_id=1, source_target_pairs={{0,8},{8,0},{1,9},{9,1},{2,10},{10,2},{3,11},{11,3},{4,12},{12,4},... | collective-permute-start | bytes 1572872 | tf_op jit(solution)/shard_map/ppermute | solution.py:18
